TPU v7x, 256 devices: a whole 4x4x8 slice. The times are simulated.
256 devices in a mesh: dp: 32 (over x, z), tensor: 8 (over y, core).
Axes of the slice: x: 4, y: 4, z: 8, core: 2. Of those that a mesh axis runs over, the one named last changes fastest.
Arguments:
- gate_pre: bfloat16 [16384, 12800], P('dp', 'tensor'), may hold values from -6 to 6
- up_pre: bfloat16 [16384, 12800], P('dp', 'tensor'), may hold values from -6 to 6
- down_codes: bfloat16 [12800, 2560], P(('tensor', 'dp')), may hold values from -127 to 127
- down_scales: float32 [12800, 10], P(('tensor', 'dp')), may hold values from 4e-05 to 0.00024
- cotangent: bfloat16 [16384, 2560], P(('dp', 'tensor')), may hold values from -6 to 6
Outputs:
- layer_out: bfloat16 [16384, 2560], P(('dp', 'tensor'))
- gate_grad: bfloat16 [16384, 12800], P('dp', 'tensor')
- up_grad: bfloat16 [16384, 12800], P('dp', 'tensor')
- weight_grad: float32 [12800, 2560], P(('tensor', 'dp'))
All inputs are finite; a program needn't handle non-finite values.
Results may differ from a plain program's by a relative error of at most 0.022.
Values may be sent and summed in bfloat16 or wider, within the bound.
A program may use at most 192 MiB of HBM per device.

v0:
```python
import jax
import jax.numpy as jnp
from jax import lax
from jax.sharding import PartitionSpec as P


def silu_parts(gate_value):
    sigmoid_gate = jax.nn.sigmoid(gate_value)
    return (gate_value * sigmoid_gate, sigmoid_gate)


def dequantize(code_block, scales):
    row_count, full_width = code_block.shape
    nblocks = scales.shape[1]
    blocks = (
        code_block.astype(jnp.float32).reshape(row_count, nblocks, full_width // nblocks)
        * scales[:, :, None]
    )
    return blocks.reshape(row_count, full_width).astype(jnp.bfloat16)


def quantize_rows(hidden, received, nblocks):
    block_count = 4
    row_span = hidden.shape[1] // block_count
    full_width = received.shape[1]
    stacked = jnp.moveaxis(hidden.reshape(hidden.shape[0], block_count, row_span), 1, 0)

    def one_block(columns):
        partial_value = lax.dot_general(
            columns, received, (((0,), (0,)), ((), ())), preferred_element_type=jnp.float32
        )
        blocks = partial_value.reshape(row_span, nblocks, full_width // nblocks)
        scale_rows = (jnp.max(jnp.abs(blocks), axis=2) + 1e-06) / 127.0
        grad_codes = (blocks / scale_rows[:, :, None]).astype(jnp.bfloat16)
        return (grad_codes.reshape(row_span, full_width), scale_rows)

    grad_codes, scale_rows = lax.map(one_block, stacked)
    return (grad_codes.reshape(-1, full_width), scale_rows.reshape(-1, nblocks))


def body(gate_pre, up_pre, down_codes, down_scales, cotangent):
    group_rows, local_hidden = gate_pre.shape
    full_width = down_codes.shape[1]
    nblocks = down_scales.shape[1]
    gate_value = gate_pre.astype(jnp.float32)
    up_value = up_pre.astype(jnp.float32)
    activated, sigmoid_gate = silu_parts(gate_value)
    hidden = (activated * up_value).astype(jnp.bfloat16)
    codes_whole, scales_whole = (
        lax.all_gather(down_codes, "dp", axis=0, tiled=True),
        lax.all_gather(down_scales.astype(jnp.bfloat16), "dp", axis=0, tiled=True).astype(
            down_scales.dtype
        ),
    )
    weight = dequantize(codes_whole, scales_whole)
    partial_value = jnp.dot(hidden, weight, preferred_element_type=jnp.float32)
    totals = lax.psum(partial_value.astype(jnp.bfloat16), "tensor").astype(jnp.float32)
    own_rows = group_rows // lax.axis_size("tensor")
    mine = lax.dynamic_slice_in_dim(totals, lax.axis_index("tensor") * own_rows, own_rows, 0)
    layer_out = mine.astype(jnp.bfloat16)
    received = lax.all_gather(cotangent, "tensor", axis=0, tiled=True)
    dhidden = lax.dot_general(
        received, weight, (((1,), (1,)), ((), ())), preferred_element_type=jnp.float32
    )
    gate_grad = (
        dhidden * up_value * sigmoid_gate * (1.0 + gate_value * (1.0 - sigmoid_gate))
    ).astype(jnp.bfloat16)
    up_grad = (dhidden * activated).astype(jnp.bfloat16)
    grad_codes, scale_rows = quantize_rows(hidden, received, nblocks)
    owners = lax.axis_size("dp")
    owned_rows = local_hidden // owners
    codes_in, scales_in = (
        lax.all_to_all(
            grad_codes.reshape(owners, owned_rows, full_width),
            "dp",
            split_axis=0,
            concat_axis=0,
            tiled=True,
        ),
        lax.all_to_all(
            scale_rows.reshape(owners, owned_rows, nblocks).astype(jnp.bfloat16),
            "dp",
            split_axis=0,
            concat_axis=0,
            tiled=True,
        ).astype(jnp.float32),
    )
    terms = (
        codes_in.astype(jnp.float32).reshape(owners, owned_rows, nblocks, full_width // nblocks)
        * scales_in[:, :, :, None]
    )
    total_tokens = group_rows * owners
    weight_grad = jnp.sum(terms, axis=0).reshape(owned_rows, full_width) * float(total_tokens) ** (
        -0.5
    )
    return (layer_out, gate_grad, up_grad, weight_grad)


def solution(mesh):
    return jax.shard_map(
        body,
        mesh=mesh,
        in_specs=(
            P("dp", "tensor"),
            P("dp", "tensor"),
            P(("tensor", "dp"), None),
            P(("tensor", "dp"), None),
            P(("dp", "tensor"), None),
        ),
        out_specs=(
            P(("dp", "tensor"), None),
            P("dp", "tensor"),
            P("dp", "tensor"),
            P(("tensor", "dp"), None),
        ),
        check_vma=False,
    )
```

profile of v0, /device:TPU:1, one launch (start us, length us, event | category | flops | bytes accessed | tf_op | source)
XLA Modules:
  0.0 488.8 jit_solution(5638897918586651270)
XLA Ops:
  9.4 38.6 %all-gather.1 = bf16[32,50,10]{1,2,0:T(8,128)(2,1)S(1)} all-gather(bf16[1,50,10]{1,2,0:T(8,128)(2,1)S(1)} %convert_bitcast_fusion), channel_id=1, replica_groups=mesh['dp'=32,'tensor'=8] {'dp'}, dimensions={0}, use_global_device_ids=true | all-gather | bytes 33000 | tf_op jit(solution)/shard_map/all_gather | solution.py:51
  48.2 6.9 %mul.54 = f32[1600,10,256]{0,2,1:T(8,128)} broadcast(f32[1600,10]{0,1:T(8,128)S(1)} %reshape.50), dimensions={0,1} | broadcast | bytes 16448000 | tf_op jit(solution)/shard_map/mul | solution.py:16
  55.1 18.7 %copy.29 = f32[1600,2560]{1,0:T(8,128)} copy(f32[1600,2560]{0,1:T(8,128)} %bitcast.51) | data formatting | bytes 32768000 | tf_op jit(solution)/shard_map/mul | solution.py:16
  73.8 3.0 copy.30
  76.8 70.5 %all-gather.7.cloned.1.call-done = bf16[32,50,2560]{2,1,0:T(8,128)(2,1)} async-done(((bf16[1,50,2560]{2,1,0:T(8,128)(2,1)}), bf16[32,50,2560]{2,1,0:T(8,128)(2,1)}) %all-gather.7.cloned.1.call-update) | async-done | bytes 8192016 | tf_op jit(solution)/shard_map/all_gather | solution.py:50
  147.3 11.0 %reshape.49 = f32[1600,2560]{1,0:T(8,128)} reshape(bf16[32,50,2560]{2,1,0:T(8,128)(2,1)} %all-gather.7.cloned.1.call-done) | data formatting | bytes 24576000 | tf_op jit(solution)/shard_map/convert_element_type | solution.py:16
  158.2 11.3 %multiply_convert_fusion = bf16[1600,2560]{1,0:T(8,128)(2,1)S(1)} fusion(f32[1600,2560]{1,0:T(8,128)} %reshape.49, f32[1600,2560]{1,0:T(8,128)} %copy.29), kind=kLoop, calls=%fused_computation.11 | loop fusion | flops 8192000 | bytes 40960000 | tf_op jit(solution)/shard_map/convert_element_type | solution.py:19
  170.3 7.5 %fusion.13 = (bf16[512,1600]{0,1:T(8,128)(2,1)}, bf16[512,1600]{0,1:T(8,128)(2,1)}, bf16[512,1600]{0,1:T(8,128)(2,1)}) fusion(bf16[512,1600]{0,1:T(8,128)(2,1)S(1)} %copy-done.5, bf16[512,1600]{0,1:T(8,128)(2,1)S(1)} %copy-done.6, bf16[1600,2560]{1,0:T(8,128)(2,1)S(1)} %multiply_convert_fusion, bf16[512,2560]{1,0:T(8,128)(2,1)S(1)} %copy-done.3), kind=kOutput, calls=%fused_computation.27 | convolution fusion | flops 4208230400 | bytes 19005440 | tf_op jit(solution)/shard_map/dot_general | solution.py:62
  177.8 52.8 %while.12 = (s32[]{:T(128)}, bf16[4,400,2560]{2,1,0:T(8,128)(2,1)}, bf16[4,400,10]{1,2,0:T(8,128)(2,1)S(1)}, bf16[4,512,400]{1,2,0:T(8,128)(2,1)}, bf16[512,2560]{0,1:T(8,128)(2,1)S(1)}, /*index=5*/s32[]{:T(128)}) while((s32[]{:T(128)}, bf16[4,400,2560]{2,1,0:T(8,128)(2,1)}, bf16[4,400,10]{1,2,0:T(8,128)(2,1)S(1)}, ...), condition=%wide.region_3.4_spmd, body=%wide.region_1.3_spmd.sunk | while | flops 1052684032 | bytes 46660240 | solution.py:37
  182.4 2.9 copy.48
  187.8 3.1 constant_dynamic-update-slice_fusion.2
  201.1 3.1 constant_dynamic-update-slice_fusion.2
  208.8 2.9 copy.48
  214.3 3.1 constant_dynamic-update-slice_fusion.2
  227.5 3.2 constant_dynamic-update-slice_fusion.2
  231.6 5.4 %all-to-all-start.1 = ((bf16[32,2,250]{2,1,0:T(2,128)(2,1)}), bf16[32,2,250]{2,1,0:T(2,128)(2,1)S(1)}, u32[]{:S(2)}, u32[]{:S(2)}) async-start(bf16[32,2,250]{2,1,0:T(2,128)(2,1)} %reshape.52), calls=%async_computation.1 | async-start | bytes 65536 | tf_op jit(solution)/shard_map/all_to_all | solution.py:80
  237.0 9.7 %reshape_reshape.4 = bf16[32,50,2560]{2,1,0:T(8,128)(2,1)} reshape(bf16[4,400,2560]{2,1,0:T(8,128)(2,1)} %get-tuple-element.32) | data formatting | bytes 16384000 | tf_op jit(solution)/shard_map/reshape;reshape | solution.py:74
  246.8 9.5 %all-to-all-start = ((bf16[32,50,2560]{2,1,0:T(8,128)(2,1)}), bf16[32,50,2560]{2,1,0:T(8,128)(2,1)}, u32[]{:S(2)}, u32[]{:S(2)}) async-start(bf16[32,50,2560]{2,1,0:T(8,128)(2,1)} %reshape_reshape.4), calls=%async_computation | async-start | bytes 18350080 | tf_op jit(solution)/shard_map/all_to_all | solution.py:73
  256.5 9.6 %convolution_convert_fusion = bf16[512,2560]{1,0:T(8,128)(2,1)} fusion(bf16[512,1600]{0,1:T(8,128)(2,1)S(1)} %bitcast.53, bf16[1600,2560]{1,0:T(8,128)(2,1)} %copy-done.2), kind=kOutput, calls=%fused_computation.15 | convolution fusion | flops 4195614720 | bytes 12451840 | tf_op jit(solution)/shard_map/dot_general | solution.py:56
  267.1 9.5 %mul.63 = f32[32,50,10,256]{3,2,0,1:T(8,128)} broadcast(f32[32,50,10]{2,0,1:T(8,128)S(1)} %copy.35), dimensions={0,1,2} | broadcast | bytes 16448000 | tf_op jit(solution)/shard_map/mul | solution.py:89
  276.6 22.1 %mul.64 = f32[32,50,2560]{2,0,1:T(8,128)} reshape(f32[32,50,10,256]{3,2,0,1:T(8,128)} %mul.63) | data formatting | bytes 32768000 | tf_op jit(solution)/shard_map/mul | solution.py:89
  298.8 42.2 %all-reduce.2.cloned.1.call-done = bf16[512,2560]{1,0:T(8,128)(2,1)} async-done(((bf16[512,2560]{1,0:T(8,128)(2,1)}), bf16[512,2560]{1,0:T(8,128)(2,1)}) %all-reduce.2.cloned.1.call-update) | async-done | bytes 2621456 | tf_op jit(solution)/shard_map/psum | solution.py:57
  342.7 120.5 %all-to-all-done = bf16[32,50,2560]{2,1,0:T(8,128)(2,1)} async-done(((bf16[32,50,2560]{2,1,0:T(8,128)(2,1)}), bf16[32,50,2560]{2,1,0:T(8,128)(2,1)}, u32[]{:S(2)}, u32[]{:S(2)}) %all-to-all-start) | async-done | bytes 8192032 | tf_op jit(solution)/shard_map/all_to_all | solution.py:73
  463.2 18.2 %fusion.4 = f32[50,2560]{1,0:T(8,128)S(1)} fusion(f32[32,50,2560]{2,0,1:T(8,128)} %mul.64, bf16[32,50,2560]{2,1,0:T(8,128)(2,1)} %all-to-all-done), kind=kLoop, calls=%fused_computation.10 | loop fusion | flops 12160000 | bytes 25088000 | tf_op jit(solution)/shard_map/reduce_sum | solution.py:93
  (70 shorter events, 42.2 us)
Async XLA Ops:
  7.2 66.6 %all-gather.5.cloned.1.call-start = ((), (), s32[]{:S(2)}) async-start(), calls=%async_computation.3 | async-start | bytes 2949120 | tf_op jit(solution)/shard_map/all_gather | solution.py:61
  7.9 139.4 %all-gather.7.cloned.1.call-start = ((), (), s32[]{:S(2)}) async-start(), calls=%async_computation.4 | async-start | bytes 9461760 | tf_op jit(solution)/shard_map/all_gather | solution.py:50
  158.2 11.3 %copy-start.3 = (bf16[512,2560]{1,0:T(8,128)(2,1)S(1)}, bf16[512,2560]{1,0:T(8,128)(2,1)}, u32[]{:S(2)}) copy-start(bf16[512,2560]{1,0:T(8,128)(2,1)} %all-gather.5.cloned.1.call-done) | copy-start | bytes 7864324
  158.2 11.6 %copy-start.5 = (bf16[512,1600]{0,1:T(8,128)(2,1)S(1)}, bf16[512,1600]{0,1:T(8,128)(2,1)}, u32[]{:S(2)}) copy-start(bf16[512,1600]{0,1:T(8,128)(2,1)} %param.7) | copy-start | bytes 4915204
  158.2 12.1 %copy-start.6 = (bf16[512,1600]{0,1:T(8,128)(2,1)S(1)}, bf16[512,1600]{0,1:T(8,128)(2,1)}, u32[]{:S(2)}) copy-start(bf16[512,1600]{0,1:T(8,128)(2,1)} %param.8) | copy-start | bytes 4915204
  170.3 7.5 %copy-start.2 = (bf16[1600,2560]{1,0:T(8,128)(2,1)}, bf16[1600,2560]{1,0:T(8,128)(2,1)S(1)}, u32[]{:S(2)}) copy-start(bf16[1600,2560]{1,0:T(8,128)(2,1)S(1)} %multiply_convert_fusion) | copy-start | bytes 24576004
  177.8 2.8 copy-start
  187.8 3.2 copy-start.1
  191.0 2.8 copy-start
  201.0 3.2 copy-start.1
  204.2 2.8 copy-start
  214.3 3.2 copy-start.1
  217.4 2.8 copy-start
  227.5 3.2 copy-start.1
  231.6 15.1 %all-to-all-start.1 = ((bf16[32,2,250]{2,1,0:T(2,128)(2,1)}), bf16[32,2,250]{2,1,0:T(2,128)(2,1)S(1)}, u32[]{:S(2)}, u32[]{:S(2)}) async-start(bf16[32,2,250]{2,1,0:T(2,128)(2,1)} %reshape.52), calls=%async_computation.1 | async-start | bytes 65536 | tf_op jit(solution)/shard_map/all_to_all | solution.py:80
  246.8 9.7 %copy-start.4 = (bf16[4,512,400]{1,2,0:T(8,128)(2,1)S(1)}, bf16[4,512,400]{1,2,0:T(8,128)(2,1)}, u32[]{:S(2)}) copy-start(bf16[4,512,400]{1,2,0:T(8,128)(2,1)} %get-tuple-element.121) | copy-start | bytes 4915204
  246.8 216.4 %all-to-all-start = ((bf16[32,50,2560]{2,1,0:T(8,128)(2,1)}), bf16[32,50,2560]{2,1,0:T(8,128)(2,1)}, u32[]{:S(2)}, u32[]{:S(2)}) async-start(bf16[32,50,2560]{2,1,0:T(8,128)(2,1)} %reshape_reshape.4), calls=%async_computation | async-start | bytes 18350080 | tf_op jit(solution)/shard_map/all_to_all | solution.py:73
  256.2 84.7 %all-reduce.2.cloned.1.call-start = ((), (), s32[]{:S(2)}) async-start(), calls=%async_computation.2 | async-start | bytes 5242880 | tf_op jit(solution)/shard_map/psum | solution.py:57
Sparse Core Ops, SparseCore 0:
  9.8 32.9 all-gather.4
  45.4 101.8 all-gather.6
  266.2 74.6 all-reduce.1
where the time goes:
time: 491 us; the launch traced here: 489 us
  waiting for transfers between devices  235 us (48%)
  local copies, waits for them, and re-layouts  118 us (24%)
  other arithmetic  39.8 us (8%)
  blocking collectives  38.6 us (8%)
  matrix products  28.3 us (6%)
  starting transfers between devices  15.1 us (3%)
  between operations  13.9 us (3%)
    all_to_all x1, waiting for transfers between devices, body(): lax.all_to_all(grad_codes.reshape(owners, owned_rows, full_width), 'dp',...  121 us
    all_gather x1, waiting for transfers between devices, body(): lax.all_gather(down_codes, 'dp', axis=0, tiled=True)  70.5 us
    psum x1, waiting for transfers between devices, body(): lax.psum(partial_value.astype(jnp.bfloat16), 'tensor').astype(jnp.float32)  42.2 us
    all_gather x1, blocking collectives, body(): lax.all_gather(down_scales.astype(jnp.bfloat16), 'dp', axis=0, tiled=True)  38.6 us
    mul x2, local copies, waits for them, and re-layouts, body(): codes_in.astype(jnp.float32)  31.7 us
    mul x2, local copies, waits for them, and re-layouts, dequantize(): code_block.astype(jnp.float32)  25.6 us
    dynamic_update_slice x8, local copies, waits for them, and re-layouts, quantize_rows(): grad_codes, scale_rows = lax.map(one_block, stacked)  22.8 us
    reduce_sum x1, other arithmetic, body(): jnp.sum(terms, axis=0).reshape(owned_rows, full_width)  18.2 us
  transfers between devices with their start and end apart: 5, of which 3 were waited for; matrix products, arithmetic and copies ran while one was open for 17% of the time, Pallas kernels for 0%

commit v1 on v0

v1 whole, which is shorter than its diff:
```python
import jax
import jax.numpy as jnp
from jax import lax
from jax.experimental import pallas as pl
from jax.experimental.pallas import tpu as pltpu
from jax.sharding import PartitionSpec as P

MESH = pl.DeviceIdType.MESH
BF = jnp.bfloat16
F32 = jnp.float32
D = 2560
TOK = 512
UNITS = 1600
WIN = 896
WR = 1008
AR, BR = 576, 432
NSEM = 160
SCALE = float(16384) ** -0.5
ORDER = (4, 3, -3, 2, -2, 1, -1, 0)


def dot(a, b):
    return jnp.dot(a, b, preferred_element_type=F32)


def dot_nt(a, b):
    return lax.dot_general(a, b, (((1,), (1,)), ((), ())), preferred_element_type=F32)


def kernel(
    gate_hbm, up_hbm, codes_ref, scales_ref, cot_in,
    out_ref, gg_ref, ug_ref, wg_ref,
    gate, up, wire, stage, w, cot, hid, hraw, hs, hst, st, g, x_in, ra, rb, fq, fb, res, stage2, stage3,
    lp, lc, ly, lf, lz, lq, dh, dd, dr, ssem, rsem, lsem,
):
    dp, t = lax.axis_index("dp"), lax.axis_index("tensor")
    x, z, y, c = dp // 8, dp % 8, t // 2, t % 2
    half = x // 2
    xb = x % 2
    is_r = c == half
    not_r = c != half
    vb = jnp.where(is_r, xb, 1 - xb)
    zdev = {1: (8 * x + (z + 1) % 8, t), -1: (8 * x + (z + 7) % 8, t)}
    ydev = {1: (dp, 2 * ((y + 1) % 4) + c), -1: (dp, 2 * ((y + 3) % 4) + c)}
    core = (dp, 2 * y + 1 - c)
    qdev = (8 * (x + 1 - 2 * xb) + z, t)
    pdp = 8 * (3 - x) + z
    psame = (pdp, t)
    pother = (pdp, 2 * y + 1 - c)
    pcore = ((pdp, 2 * y), (pdp, 2 * y + 1))

    count = [0]

    def rc(src, dst, dev):
        i = count[0]
        count[0] += 1
        return pltpu.make_async_remote_copy(
            src_ref=src, dst_ref=dst, send_sem=ssem.at[i], recv_sem=rsem.at[i],
            device_id=dev, device_id_type=MESH,
        )

    sent = []

    def start(cp):
        cp.start()
        sent.append(cp)

    load_gate = pltpu.make_async_copy(gate_hbm, gate, lsem.at[0])
    load_up = pltpu.make_async_copy(up_hbm, up, lsem.at[1])
    load_gate.start()
    load_up.start()

    barrier = pltpu.get_barrier_semaphore()
    everyone = (zdev[1], zdev[-1], ydev[1], ydev[-1], core, qdev, psame, pother)
    for dev in everyone:
        pl.semaphore_signal(barrier, inc=1, device_id=dev, device_id_type=MESH)

    left = []
    for p in range(20):
        scale = scales_ref[:, p // 2 : p // 2 + 1]
        piece = codes_ref[:, 128 * p : 128 * p + 128].astype(F32) * scale
        stage[48 * p : 48 * p + 48, :] = piece[:48].astype(BF)
        left.append(piece[48:50])
    left.append(jnp.zeros((8, 128), F32))
    stage[960:1008, :] = jnp.concatenate(left, axis=0).astype(BF)

    pl.semaphore_wait(barrier, len(everyone))

    def blk(b, k):
        return 8 * b + lax.rem(z + k + 8, 8)

    rows_a = pl.ds(0, AR)
    rows_b = pl.ds(AR, BR)
    half_a = {1: pl.ds(0, 288), -1: pl.ds(288, 288)}
    half_b = {1: pl.ds(AR, 224), -1: pl.ds(AR + 224, 208)}
    own_slot = 8 * vb + z

    swap_w = rc(stage, wire.at[8 * xb + z], pother)
    own_w = pltpu.make_async_copy(stage, wire.at[own_slot], lsem.at[2])

    def ring(b, rows, halves):
        return {
            (d, s): rc(
                wire.at[blk(b, -d * (s - 1)), rows if s < 4 else halves[d]],
                wire.at[blk(b, -d * (s - 1)), rows if s < 4 else halves[d]],
                zdev[d],
            )
            for s in (1, 2, 3, 4)
            for d in (1, -1)
        }

    fa = ring(vb, rows_a, half_a)
    fb_own = ring(vb, rows_b, half_b)
    fb_q = ring(1 - vb, rows_b, half_b)
    q_b = rc(wire.at[own_slot, rows_b], wire.at[own_slot, rows_b], qdev)
    q_a = {
        k: rc(wire.at[blk(vb, k), rows_a], wire.at[blk(vb, k), rows_a], qdev)
        for k in (0, 1, -1, 2, -2, 3, -3)
    }
    for d in (1, -1):
        q_a[4, d] = rc(wire.at[blk(vb, 4), half_a[d]], wire.at[blk(vb, 4), half_a[d]], qdev)

    def ag_begin():
        for cp in (q_b, fa[1, 1], fa[-1, 1], fb_own[1, 1], fb_own[-1, 1], q_a[0]):
            cp.start()

    sent.extend((q_b, fa[1, 1], fa[-1, 1], fb_own[1, 1], fb_own[-1, 1], q_a[0]))

    def ag_a(s):
        for d in (1, -1):
            fa[d, s].wait_recv()
            if s < 4:
                start(fa[d, s + 1])
                start(q_a[-d * s])
            else:
                start(q_a[4, d])

    def ag_b(s, which):
        for d in (1, -1):
            which[d, s].wait_recv()
            if s < 4:
                start(which[d, s + 1])

    def crow(gr, tt):
        return pl.multiple_of(512 * gr + 64 * tt, 32)

    def cblk(gr, yy, off=0, n=64):
        return cot.at[pl.ds(pl.multiple_of(512 * gr + 64 * (2 * yy + c) + off, 32), n)]

    y1, ym1, y2 = (y + 1) % 4, (y + 3) % 4, (y + 2) % 4
    cot_p = rc(cot_in, cblk(1, y), psame)
    own_c = pltpu.make_async_copy(cot_in, cblk(0, y), lsem.at[3])
    cot_y, cot_h, cot_core = {}, {}, {}
    for gr in (0, 1):
        mine = cot_in if gr == 0 else cblk(1, y)
        for d in (1, -1):
            cot_y[gr, d] = rc(mine, cblk(gr, y), ydev[d])
        cot_h[gr, 1] = rc(cblk(gr, ym1, 0, 32), cblk(gr, ym1, 0, 32), ydev[1])
        cot_h[gr, -1] = rc(cblk(gr, y1, 32, 32), cblk(gr, y1, 32, 32), ydev[-1])
        cot_core[gr, 0] = rc(mine, cblk(gr, y), core)
        cot_core[gr, 1] = rc(cblk(gr, ym1), cblk(gr, ym1), core)
        cot_core[gr, -1] = rc(cblk(gr, y1), cblk(gr, y1), core)
        cot_core[gr, 2] = rc(cblk(gr, y2, 0, 32), cblk(gr, y2, 0, 32), core)
        cot_core[gr, -2] = rc(cblk(gr, y2, 32, 32), cblk(gr, y2, 32, 32), core)

    def cot_begin(gr):
        for d in (1, -1):
            start(cot_y[gr, d])
        start(cot_core[gr, 0])

    def cot_forward(gr):
        for d in (1, -1):
            cot_y[gr, d].wait_recv()
            start(cot_h[gr, d])
            start(cot_core[gr, d])

    def cot_last(gr):
        for d in (1, -1):
            cot_h[gr, d].wait_recv()
            start(cot_core[gr, 2 * d])

    def cot_end(gr):
        for k in (0, 1, -1, 2, -2):
            cot_core[gr, k].wait_recv()

    def win(h):
        return hid.at[:, 768 * h : 768 * h + WIN]

    hid_p = {h: rc(win(h), hraw.at[1], pcore[h]) for h in (0, 1)}
    hid_core = {h: rc(win(h), hraw.at[0], core) for h in (0, 1)}
    hid_own = {h: pltpu.make_async_copy(win(h), hraw.at[0], lsem.at[4]) for h in (0, 1)}

    def hidden_rows(lo, hi):
        @pl.loop(lo, hi)
        def _(i):
            r = pl.ds(pl.multiple_of(16 * i, 16), 16)
            gv = gate[r, :].astype(F32)
            uv = up[r, :].astype(F32)
            hid[r, 0:UNITS] = (gv * jax.nn.sigmoid(gv) * uv).astype(BF)
            hid[r, UNITS:1664] = jnp.zeros((16, 1664 - UNITS), BF)

    def both(fn):
        for h in (0, 1):
            pl.when(c == h)(lambda h=h: fn(h))

    @pl.when(not_r)
    def _():
        swap_w.start()

    start(cot_p)
    own_c.start()
    cot_begin(0)

    @pl.when(is_r)
    def _():
        own_w.start()
        own_w.wait()
        ag_begin()

    @pl.loop(0, 16)
    def _(b):
        row = lax.broadcasted_iota(jnp.int32, (64, WIN), 0)
        lane = lax.broadcasted_iota(jnp.int32, (64, WIN), 1)
        hit = (lane == row + (32 * c + 50 * b)) & (row < 50)
        st[pl.ds(pl.multiple_of(64 * b, 64), 64), :] = jnp.where(hit, 1.0, 0.0).astype(BF)

    load_gate.wait()
    load_up.wait()
    hidden_rows(0, 8)

    @pl.when(not_r)
    def _():
        swap_w.wait_recv()
        ag_begin()

    hidden_rows(8, 32)

    @pl.when(not_r)
    def _():
        hid_p[0].start()
        hid_p[1].start()

    @pl.when(is_r)
    def _():
        both(lambda h: hid_own[h].start())
        both(lambda h: hid_core[1 - h].start())

    def spread(gr):
        src = hraw.at[gr]
        for b, lo in ((0, 0), (512, 384)):
            sel = st[b : b + 512, lo : lo + 512]
            val = src[:, lo : lo + 512]
            hs[512 * gr : 512 * gr + 512, b : b + 512] = dot_nt(val, sel).astype(BF)
            hst[b : b + 512, 512 * gr : 512 * gr + 512] = dot_nt(sel, val).astype(BF)

    def wgrad():
        @pl.loop(0, 4)
        def _(m):
            left = [[] for _ in range(4)]
            lhs = hst[pl.ds(pl.multiple_of(256 * m, 256), 256), :]
            for n in range(5):
                acc = dot(lhs, cot[:, 512 * n : 512 * n + 512])
                for b in range(4):
                    for j in range(4):
                        p = 4 * n + j
                        col = acc[:, 128 * j : 128 * j + 128]
                        g[4 * m + b, 48 * p : 48 * p + 48, :] = col[64 * b : 64 * b + 48].astype(BF)
                        left[b].append(col[64 * b + 48 : 64 * b + 50])
            for b in range(4):
                tail = jnp.concatenate(left[b] + [jnp.zeros((8, 128), F32)], axis=0)
                g[4 * m + b, 960:1008, :] = tail.astype(BF)

    def unpack():
        @pl.loop(0, 16)
        def _(i):
            base = pl.multiple_of(64 * i, 64)
            tail = wire[i, 960:1008, :].astype(F32)
            for p in range(20):
                cols = slice(128 * p, 128 * p + 128)
                w[pl.ds(base, 48), cols] = wire[i, 48 * p : 48 * p + 48, :]
                last = jnp.concatenate([tail[2 * p : 2 * p + 2], jnp.zeros((14, 128), F32)], axis=0)
                w[pl.ds(base + 48, 16), cols] = last.astype(BF)

    def kidx(k):
        return k + 3

    ga = {k: rc(g.at[blk(1 - vb, k), rows_a], x_in.at[kidx(k)], qdev) for k in ORDER}
    ha = {1: pl.ds(0, 288), -1: pl.ds(288, 288)}
    hb = {1: pl.ds(0, 224), -1: pl.ds(224, 208)}
    ra_c, rb_c = {}, {}
    for s in (1, 2, 3, 4):
        for d in (1, -1):
            if s == 1:
                ra_c[d, s] = rc(x_in.at[kidx(4), ha[d]], ra.at[(1 - d) // 2, 0, ha[d]], zdev[d])
            else:
                ra_c[d, s] = rc(x_in.at[kidx(d * (5 - s))], ra.at[(1 - d) // 2, s - 1], zdev[d])
            for bb, b in ((0, vb), (1, 1 - vb)):
                if s == 1:
                    rb_c[bb, d, s] = rc(g.at[blk(b, 4), half_b[d]], rb.at[bb, (1 - d) // 2, 0, hb[d]], zdev[d])
                else:
                    rb_c[bb, d, s] = rc(g.at[blk(b, d * (5 - s)), rows_b], rb.at[bb, (1 - d) // 2, s - 1], zdev[d])
    fin_q = rc(fq, fb, qdev)
    swap_g = rc(stage2, stage3, pother)

    def add_into(dst, *terms):
        n = dst.shape[0]
        step = 144 if n % 144 == 0 else 16

        @pl.loop(0, n // step)
        def _(i):
            r = pl.ds(pl.multiple_of(i * step, 16), step)
            v = dst[r, :].astype(F32)
            for term in terms:
                v = v + term[r, :].astype(F32)
            dst[r, :] = v.astype(dst.dtype)

    def rs_begin():
        for bb in (1, 0):
            for d in (1, -1):
                start(rb_c[bb, d, 1])
        for k in ORDER:
            start(ga[k])

    def rs_x(k):
        ga[k].wait_recv()
        add_into(x_in.at[kidx(k)], g.at[blk(vb, k), rows_a])

    def rs_a(s):
        if s == 1:
            rs_x(4)
            for d in (1, -1):
                start(ra_c[d, 1])
            return
        for d in (1, -1):
            k = d * (5 - s)
            rs_x(k)
            ra_c[d, s - 1].wait_recv()
            rows = ha[d] if s == 2 else pl.ds(0, AR)
            add_into(x_in.at[kidx(k), rows], ra.at[(1 - d) // 2, s - 2, rows])
            start(ra_c[d, s])

    def rs_b(s):
        for bb, b in ((1, 1 - vb), (0, vb)):
            for d in (1, -1):
                k = d * (5 - s)
                rb_c[bb, d, s - 1].wait_recv()
                if s == 2:
                    dst, src = g.at[blk(b, k), half_b[d]], rb.at[bb, (1 - d) // 2, 0, hb[d]]
                else:
                    dst, src = g.at[blk(b, k), rows_b], rb.at[bb, (1 - d) // 2, s - 2]
                add_into(dst, src)
                start(rb_c[bb, d, s])

    def rs_end():
        for d in (1, -1):
            rb_c[1, d, 4].wait_recv()
        fq[...] = (
            g[blk(1 - vb, 0), rows_b, :].astype(F32)
            + rb[1, 0, 3].astype(F32)
            + rb[1, 1, 3].astype(F32)
        ).astype(BF)
        start(fin_q)
        rs_x(0)
        for d in (1, -1):
            ra_c[d, 4].wait_recv()
            rb_c[0, d, 4].wait_recv()
        res[rows_a, :] = x_in[kidx(0)].astype(F32) + ra[0, 3].astype(F32) + ra[1, 3].astype(F32)
        part = g[blk(vb, 0), rows_b, :].astype(F32) + rb[0, 0, 3].astype(F32) + rb[0, 1, 3].astype(F32)
        fin_q.wait_recv()
        res[rows_b, :] = part + fb[...].astype(F32)

        @pl.when(not_r)
        def _():
            stage2[...] = res[...].astype(BF)
            swap_g.start()
            swap_g.wait_recv()
            res[...] = stage3[...].astype(F32)
            swap_g.wait_send()

        for p in range(20):
            cols = slice(128 * p, 128 * p + 128)
            wg_ref[0:48, cols] = res[48 * p : 48 * p + 48, :] * SCALE
            wg_ref[48:50, cols] = res[960 + 2 * p : 962 + 2 * p, :] * SCALE

    def layer(gr, ch):
        @pl.loop(0, 5)
        def _(n):
            off = pl.multiple_of(256 * n, 256)
            acc = dot(hs[512 * gr : 512 * gr + 512, :], w[:, pl.ds(pl.multiple_of(1280 * ch + off, 256), 256)])
            for tt in range(8):
                r = 64 * (tt // 2)
                lp[gr, ch, tt % 2, r : r + 64, pl.ds(off, 256)] = acc[64 * tt : 64 * tt + 64].astype(BF)

    l_core, l_y1, l_y2, l_p = {}, {}, {}, {}

    def yrow(yy, off=0, n=64):
        return pl.ds(pl.multiple_of(64 * yy + off, 32), n)

    for gr in (1, 0):
        for ch in (0, 1):
            l_core[gr, ch] = rc(lp.at[gr, ch, 1 - c], lc.at[gr, ch], core)
            for d in (1, -1):
                o = 0 if d == 1 else 32
                l_y1[gr, ch, d] = rc(lc.at[gr, ch, yrow(y2, o, 32)], ly.at[gr, ch, (1 - d) // 2], ydev[d])
                to = y1 if d == 1 else ym1
                l_y2[gr, ch, d] = rc(lc.at[gr, ch, yrow(to)], lf.at[gr, ch, (1 - d) // 2], ydev[d])
    for ch in (0, 1):
        l_p[ch] = rc(lz.at[ch], lq.at[ch], psame)

    def layer_core(gr, ch):
        l_core[gr, ch].wait_recv()
        add_into(lc.at[gr, ch], lp.at[gr, ch, c])
        for d in (1, -1):
            start(l_y1[gr, ch, d])

    def layer_y(gr, ch):
        for d in (1, -1):
            l_y1[gr, ch, d].wait_recv()
            o = 0 if d == 1 else 32
            to = y1 if d == 1 else ym1
            add_into(lc.at[gr, ch, yrow(to, o, 32)], ly.at[gr, ch, (1 - d) // 2])
            start(l_y2[gr, ch, d])

    def layer_end(gr, ch):
        for d in (1, -1):
            l_y2[gr, ch, d].wait_recv()
        total = lc[gr, ch, yrow(y), :].astype(F32) + lf[gr, ch, 0].astype(F32) + lf[gr, ch, 1].astype(F32)
        if gr == 1:
            lz[ch] = total.astype(BF)
            start(l_p[ch])
        else:
            l_p[ch].wait_recv()
            out_ref[:, 1280 * ch : 1280 * ch + 1280] = (total + lq[ch].astype(F32)).astype(BF)

    d_p = {}
    d_p["same"] = {h: rc(dd.at[1], dr.at[h], psame) for h in (0, 1)}
    d_p["other"] = {h: rc(dd.at[1], dr.at[h], pother) for h in (0, 1)}
    d_core = {h: rc(dd.at[0], dr.at[h], core) for h in (0, 1)}
    d_own = {h: pltpu.make_async_copy(dd.at[0], dr.at[h], lsem.at[5]) for h in (0, 1)}

    def dhidden(gr):
        @pl.loop(0, 4)
        def _(n):
            off = pl.multiple_of(256 * n, 256)
            dh[:, pl.ds(off, 256)] = dot_nt(cot[512 * gr : 512 * gr + 512, :], w[pl.ds(off, 256), :]).astype(BF)

        a = dot(dh[:, 0:512], st[0:512, 0:512])
        b = dot(dh[:, 512:1024], st[512:1024, 384:896])
        dd[gr, :, 0:384] = a[:, 0:384].astype(BF)
        dd[gr, :, 384:512] = (a[:, 384:512] + b[:, 0:128]).astype(BF)
        dd[gr, :, 512:896] = b[:, 128:512].astype(BF)

    def d_send_p():
        @pl.when(is_r)
        def _():
            both(lambda h: d_p["same"][h].start())

        @pl.when(not_r)
        def _():
            both(lambda h: d_p["other"][h].start())

    def d_send_core():
        @pl.when(is_r)
        def _():
            both(lambda h: d_own[h].start())

        @pl.when(not_r)
        def _():
            both(lambda h: d_core[h].start())

    def d_recv():
        @pl.when(is_r)
        def _():
            both(lambda h: d_own[h].wait())
            both(lambda h: d_core[1 - h].wait_recv())

        @pl.when(not_r)
        def _():
            def arrive(h):
                d_p["same"][h].wait_recv()
                d_p["other"][1 - h].wait_recv()

            both(arrive)

    def d_sent():
        @pl.when(is_r)
        def _():
            both(lambda h: d_p["same"][h].wait_send())

        @pl.when(not_r)
        def _():
            both(lambda h: d_p["other"][h].wait_send())
            both(lambda h: d_core[h].wait_send())

    def grads():
        @pl.loop(0, 32)
        def _(i):
            r = pl.ds(pl.multiple_of(16 * i, 16), 16)

            def write(dv, lo, hi):
                gv = gate[r, lo:hi].astype(F32)
                uv = up[r, lo:hi].astype(F32)
                sv = jax.nn.sigmoid(gv)
                gg_ref[r, lo:hi] = (dv * uv * sv * (1.0 + gv * (1.0 - sv))).astype(BF)
                ug_ref[r, lo:hi] = (dv * (gv * sv)).astype(BF)

            write(dr[0, r, 0:768].astype(F32), 0, 768)
            write(dr[0, r, 768:896].astype(F32) + dr[1, r, 0:128].astype(F32), 768, 896)
            write(dr[1, r, 128:832].astype(F32), 896, 1600)

    ag_a(1)
    cot_forward(0)
    ag_b(1, fb_own)
    q_b.wait_recv()
    for d in (1, -1):
        start(fb_q[d, 1])

    cot_p.wait_recv()
    cot_begin(1)
    ag_a(2)
    cot_last(0)

    @pl.when(is_r)
    def _():
        both(lambda h: hid_own[h].wait())

    @pl.when(not_r)
    def _():
        both(lambda h: hid_core[h].wait_recv())

    spread(0)
    ag_b(2, fb_own)
    ag_b(1, fb_q)
    cot_forward(1)
    ag_a(3)
    ag_b(3, fb_own)
    ag_b(2, fb_q)
    cot_last(1)
    cot_end(0)
    cot_end(1)
    own_c.wait()
    ag_a(4)
    ag_b(4, fb_own)
    ag_b(3, fb_q)

    both(lambda h: hid_p[h].wait_recv())
    spread(1)
    ag_b(4, fb_q)
    wgrad()
    rs_begin()
    for k in (0, 1, -1, 2, -2, 3, -3):
        q_a[k].wait_recv()
    for d in (1, -1):
        q_a[4, d].wait_recv()
    unpack()
    rs_a(1)
    dhidden(1)
    d_send_p()
    rs_b(2)
    layer(1, 0)
    start(l_core[1, 0])
    rs_a(2)
    layer(1, 1)
    start(l_core[1, 1])
    layer_core(1, 0)
    rs_b(3)
    layer_core(1, 1)
    rs_a(3)
    layer_y(1, 0)
    dhidden(0)
    d_send_core()
    layer_y(1, 1)
    rs_b(4)
    layer(0, 0)
    start(l_core[0, 0])
    layer(0, 1)
    start(l_core[0, 1])
    layer_end(1, 0)
    layer_end(1, 1)
    layer_core(0, 0)
    layer_core(0, 1)
    rs_a(4)
    layer_y(0, 0)
    layer_y(0, 1)
    d_recv()
    grads()
    rs_end()
    layer_end(0, 0)
    layer_end(0, 1)

    for cp in sent:
        cp.wait_send()

    @pl.when(not_r)
    def _():
        swap_w.wait_send()
        hid_p[0].wait_send()
        hid_p[1].wait_send()

    @pl.when(is_r)
    def _():
        both(lambda h: hid_core[1 - h].wait_send())

    d_sent()


def body(gate_pre, up_pre, down_codes, down_scales, cotangent):
    vmem = pl.BlockSpec(memory_space=pltpu.VMEM)
    anywhere = pl.BlockSpec(memory_space=pl.ANY)
    return pl.pallas_call(
        kernel,
        out_shape=(
            jax.ShapeDtypeStruct((64, D), BF),
            jax.ShapeDtypeStruct((TOK, UNITS), BF),
            jax.ShapeDtypeStruct((TOK, UNITS), BF),
            jax.ShapeDtypeStruct((50, D), F32),
        ),
        in_specs=[anywhere, anywhere, vmem, vmem, vmem],
        out_specs=(vmem, vmem, vmem, vmem),
        scratch_shapes=[
            pltpu.VMEM((TOK, UNITS), BF),
            pltpu.VMEM((TOK, UNITS), BF),
            pltpu.VMEM((16, WR, 128), BF),
            pltpu.VMEM((WR, 128), BF),
            pltpu.VMEM((1024, D), BF),
            pltpu.VMEM((1024, D), BF),
            pltpu.VMEM((TOK, 1664), BF),
            pltpu.VMEM((2, TOK, WIN), BF),
            pltpu.VMEM((1024, 1024), BF),
            pltpu.VMEM((1024, 1024), BF),
            pltpu.VMEM((1024, WIN), BF),
            pltpu.VMEM((16, WR, 128), BF),
            pltpu.VMEM((8, AR, 128), BF),
            pltpu.VMEM((2, 4, AR, 128), BF),
            pltpu.VMEM((2, 2, 4, BR, 128), BF),
            pltpu.VMEM((BR, 128), BF),
            pltpu.VMEM((BR, 128), BF),
            pltpu.VMEM((WR, 128), F32),
            pltpu.VMEM((WR, 128), BF),
            pltpu.VMEM((WR, 128), BF),
            pltpu.VMEM((2, 2, 2, 256, 1280), BF),
            pltpu.VMEM((2, 2, 256, 1280), BF),
            pltpu.VMEM((2, 2, 2, 32, 1280), BF),
            pltpu.VMEM((2, 2, 2, 64, 1280), BF),
            pltpu.VMEM((2, 64, 1280), BF),
            pltpu.VMEM((2, 64, 1280), BF),
            pltpu.VMEM((TOK, 1024), BF),
            pltpu.VMEM((2, TOK, WIN), BF),
            pltpu.VMEM((2, TOK, WIN), BF),
            pltpu.SemaphoreType.DMA((NSEM,)),
            pltpu.SemaphoreType.DMA((NSEM,)),
            pltpu.SemaphoreType.DMA((8,)),
        ],
        compiler_params=pltpu.CompilerParams(
            collective_id=0, has_side_effects=True, vmem_limit_bytes=62 << 20
        ),
        cost_estimate=pl.CostEstimate(flops=25_000_000_000, bytes_accessed=10_000_000, transcendentals=2_000_000),
    )(gate_pre, up_pre, down_codes, down_scales, cotangent)


def solution(mesh):
    return jax.shard_map(
        body,
        mesh=mesh,
        in_specs=(
            P("dp", "tensor"),
            P("dp", "tensor"),
            P(("tensor", "dp"), None),
            P(("tensor", "dp"), None),
            P(("dp", "tensor"), None),
        ),
        out_specs=(
            P(("dp", "tensor"), None),
            P("dp", "tensor"),
            P("dp", "tensor"),
            P(("tensor", "dp"), None),
        ),
        check_vma=False,
    )
```

time: 491 us -> 122 us (0.25)
  waiting for transfers between devices: 235 us -> 0 us
  Pallas kernels: 0 us -> 106 us
  local copies, waits for them, and re-layouts: 118 us -> 15.1 us
  other arithmetic: 39.8 us -> 0 us
  blocking collectives: 38.6 us -> 0 us
  matrix products: 28.3 us -> 0 us
  starting transfers between devices: 15.1 us -> 0 us
  between operations: 13.9 us -> 0.66 us
    all_to_all x2 -> x0, waiting for transfers between devices: 121 us -> none  [the longest x1 121 us: body(): lax.all_to_all(grad_codes.reshape(owners, owned_rows, full_width), 'dp',...]
    pallas_call x0 -> x1, Pallas kernels: none -> 106 us  [body(): pl.pallas_call(kernel, out_shape=(jax.ShapeDtypeStruct((64, D), BF), jax....]
    all_gather x2 -> x0, waiting for transfers between devices: 70.5 us -> none  [the longest x1 70.5 us: body(): lax.all_gather(down_codes, 'dp', axis=0, tiled=True)]
    mul x4 -> x0, local copies, waits for them, and re-layouts: 57.2 us -> none  [the longest x2 31.7 us: body(): codes_in.astype(jnp.float32)]
    psum x1 -> x0, waiting for transfers between devices: 42.2 us -> none  [body(): lax.psum(partial_value.astype(jnp.bfloat16), 'tensor').astype(jnp.float32)]
    all_gather x1 -> x0, blocking collectives: 38.6 us -> none  [body(): lax.all_gather(down_scales.astype(jnp.bfloat16), 'dp', axis=0, tiled=True)]
    dot_general x6 -> x0, matrix products: 28.3 us -> none  [the longest x4 11.2 us: one_block(): lax.dot_general(columns, received, (((0,), (0,)), ((), ())), preferred_el...]
    convert_element_type x10 -> x0, local copies, waits for them, and re-layouts: 23.6 us -> none  [the longest x4 11.5 us: one_block(): grad_codes = (blocks / scale_rows[:, :, None]).astype(jnp.bfloat16)]
  transfers between devices with their start and end apart: 5 -> 0, of which waited for: 3 -> 0; matrix products, arithmetic and copies ran while one was open for 17% -> 0% of each run, Pallas kernels for 0% -> 0%
where the time goes in v1:
time: 122 us
  Pallas kernels  106 us (87%)
  local copies, waits for them, and re-layouts  15.1 us (12%)
    pallas_call x1, Pallas kernels, body(): pl.pallas_call(kernel, out_shape=(jax.ShapeDtypeStruct((64, D), BF), jax....  106 us
    unnamed x13, local copies, waits for them, and re-layouts  9.08 us
    pallas_call x2, local copies, waits for them, and re-layouts, body(): pl.pallas_call(kernel, out_shape=(jax.ShapeDtypeStruct((64, D), BF), jax....  5.98 us

profile of v1, /device:TPU:1, one launch (start us, length us, event | category | flops | bytes accessed | tf_op | source)
XLA Modules:
  0.0 122.2 jit_solution(12661744818228392433)
XLA Ops:
  0.6 0.0 copy-start.1
  0.6 1.5 %copy.11.scales_ref = f32[50,10]{1,0:T(8,128)} copy(f32[50,10]{0,1:T(8,128)} %param.8) | data formatting | bytes 4000 | tf_op args[3]
  2.2 3.6 %copy.9.gate_hbm = bf16[512,1600]{1,0:T(8,128)(2,1)} copy(bf16[512,1600]{0,1:T(8,128)(2,1)} %param.5) | data formatting | bytes 3276800 | tf_op args[0]
  5.8 0.0 copy-done.1
  5.8 2.4 %copy.10.up_hbm = bf16[512,1600]{1,0:T(8,128)(2,1)} copy(bf16[512,1600]{0,1:T(8,128)(2,1)S(1)} %copy-done.1) | data formatting | bytes 3276800 | tf_op args[1]
  8.2 106.4 %shard_map.84 = (bf16[64,2560]{1,0:T(8,128)(2,1)}, bf16[512,1600]{1,0:T(8,128)(2,1)}, bf16[512,1600]{1,0:T(8,128)(2,1)}, f32[50,2560]{1,0:T(8,128)}) custom-call(bf16[512,1600]{1,0:T(8,128)(2,1)} %copy.9.gate_hbm, bf16[512,1600]{1,0:T(8,128)(2,1)} %copy.10.up_hbm, bf16[50,2560]{1,0:T(8,128)(2,1)} %codes_ref.1, f32[50,10]{1,0:T(8,128)} %copy.11.scales_ref, ...), custom_call_target="tpu_custom_call" | custom-call | flops 24999999488 | bytes 10000000 | tf_op jit(solution)/shard_map/pallas_call | solution.py:610
  114.6 0.0 copy-start
  114.6 3.7 %copy.12 = bf16[512,1600]{0,1:T(8,128)(2,1)} copy(bf16[512,1600]{1,0:T(8,128)(2,1)} %get-tuple-element.5) | data formatting | bytes 3276800 | tf_op jit(solution)/shard_map/pallas_call | solution.py:610
  118.4 0.0 copy-done
  118.4 0.0 copy-start.3
  118.4 0.0 copy-start.2
  118.4 2.3 %copy.13 = bf16[512,1600]{0,1:T(8,128)(2,1)} copy(bf16[512,1600]{1,0:T(8,128)(2,1)S(1)} %copy-done) | data formatting | bytes 3276800 | tf_op jit(solution)/shard_map/pallas_call | solution.py:610
  120.6 0.0 copy-done.3
  120.6 0.7 copy.16
  121.4 0.0 copy-done.2
  121.4 0.8 copy.17
Async XLA Ops:
  0.6 5.1 %copy-start.1 = (bf16[512,1600]{0,1:T(8,128)(2,1)S(1)}, bf16[512,1600]{0,1:T(8,128)(2,1)}, u32[]{:S(2)}) copy-start(bf16[512,1600]{0,1:T(8,128)(2,1)} %param.6) | copy-start | bytes 4915204
  114.6 3.7 %copy-start = (bf16[512,1600]{1,0:T(8,128)(2,1)S(1)}, bf16[512,1600]{1,0:T(8,128)(2,1)}, u32[]{:S(2)}) copy-start(bf16[512,1600]{1,0:T(8,128)(2,1)} %get-tuple-element.6) | copy-start | bytes 4915204
  118.4 2.3 %copy-start.3 = (bf16[64,2560]{1,0:T(8,128)(2,1)S(1)}, bf16[64,2560]{1,0:T(8,128)(2,1)}, u32[]{:S(2)}) copy-start(bf16[64,2560]{1,0:T(8,128)(2,1)} %get-tuple-element.12) | copy-start | bytes 983044
  118.4 3.0 %copy-start.2 = (f32[50,2560]{1,0:T(8,128)S(1)}, f32[50,2560]{1,0:T(8,128)}, u32[]{:S(2)}) copy-start(f32[50,2560]{1,0:T(8,128)} %get-tuple-element.15) | copy-start | bytes 1536004

commit v2 on v1

v2 whole, which is shorter than its diff:
```python
import jax
import jax.numpy as jnp
from jax import lax
from jax.experimental import pallas as pl
from jax.experimental.pallas import tpu as pltpu
from jax.sharding import PartitionSpec as P

MESH = pl.DeviceIdType.MESH
BF = jnp.bfloat16
F32 = jnp.float32
D = 2560
TOK = 512
UNITS = 1600
HALF = 800
WR = 1008
AR, BR = 576, 432
AG, BG = 480, 528
NSEM = 160
SCALE = float(16384) ** -0.5
ORDER = (4, 3, -3, 2, -2, 1, -1, 0)


def dot(a, b):
    return jnp.dot(a, b, preferred_element_type=F32)


def dot_nt(a, b):
    return lax.dot_general(a, b, (((1,), (1,)), ((), ())), preferred_element_type=F32)


def kernel(
    gate_hbm, up_hbm, codes_ref, scales_ref, cot_in,
    out_ref, dr, res,
    gate, up, wire, stage, w, cot, hid, ht, hs, eye, g, x_in, ra, rb, fq, fb, stage2, stage3,
    lp, lc, ly, lf, lz, lq, dd, ssem, rsem, lsem,
):
    dp, t = lax.axis_index("dp"), lax.axis_index("tensor")
    x, z, y, c = dp // 8, dp % 8, t // 2, t % 2
    half = x // 2
    xb = x % 2
    is_r = c == half
    not_r = c != half
    vb = jnp.where(is_r, xb, 1 - xb)
    zdev = {1: (8 * x + (z + 1) % 8, t), -1: (8 * x + (z + 7) % 8, t)}
    ydev = {1: (dp, 2 * ((y + 1) % 4) + c), -1: (dp, 2 * ((y + 3) % 4) + c)}
    core = (dp, 2 * y + 1 - c)
    qdev = (8 * (x + 1 - 2 * xb) + z, t)
    pdp = 8 * (3 - x) + z
    psame = (pdp, t)
    pother = (pdp, 2 * y + 1 - c)
    pcore = ((pdp, 2 * y), (pdp, 2 * y + 1))

    count = [0]

    def rc(src, dst, dev):
        i = count[0]
        count[0] += 1
        return pltpu.make_async_remote_copy(
            src_ref=src, dst_ref=dst, send_sem=ssem.at[i], recv_sem=rsem.at[i],
            device_id=dev, device_id_type=MESH,
        )

    sent = []

    def start(cp):
        cp.start()
        sent.append(cp)

    load_gate = pltpu.make_async_copy(gate_hbm, gate, lsem.at[0])
    load_up = pltpu.make_async_copy(up_hbm, up, lsem.at[1])
    load_gate.start()
    load_up.start()

    barrier = pltpu.get_barrier_semaphore()
    everyone = (zdev[1], zdev[-1], ydev[1], ydev[-1], core, qdev, psame, pother)
    for dev in everyone:
        pl.semaphore_signal(barrier, inc=1, device_id=dev, device_id_type=MESH)

    left = []
    for p in range(20):
        scale = scales_ref[:, p // 2 : p // 2 + 1]
        piece = codes_ref[:, 128 * p : 128 * p + 128].astype(F32) * scale
        stage[48 * p : 48 * p + 48, :] = piece[:48].astype(BF)
        left.append(piece[48:50])
    left.append(jnp.zeros((8, 128), F32))
    stage[960:1008, :] = jnp.concatenate(left, axis=0).astype(BF)

    pl.semaphore_wait(barrier, len(everyone))

    def blk(b, k):
        return 8 * b + lax.rem(z + k + 8, 8)

    rows_a = slice(0, AR)
    rows_b = slice(AR, WR)
    half_a = {1: pl.ds(0, 288), -1: pl.ds(288, 288)}
    half_b = {1: pl.ds(AR, 224), -1: pl.ds(AR + 224, 208)}
    own_slot = 8 * vb + z

    swap_w = rc(stage, wire.at[8 * xb + z], pother)
    own_w = pltpu.make_async_copy(stage, wire.at[own_slot], lsem.at[2])

    def ring(b, rows, halves):
        return {
            (d, s): rc(
                wire.at[blk(b, -d * (s - 1)), rows if s < 4 else halves[d]],
                wire.at[blk(b, -d * (s - 1)), rows if s < 4 else halves[d]],
                zdev[d],
            )
            for s in (1, 2, 3, 4)
            for d in (1, -1)
        }

    fa = ring(vb, rows_a, half_a)
    fb_own = ring(vb, rows_b, half_b)
    fb_q = ring(1 - vb, rows_b, half_b)
    q_b = rc(wire.at[own_slot, rows_b], wire.at[own_slot, rows_b], qdev)
    q_a = {
        k: rc(wire.at[blk(vb, k), rows_a], wire.at[blk(vb, k), rows_a], qdev)
        for k in (0, 1, -1, 2, -2, 3, -3)
    }
    for d in (1, -1):
        q_a[4, d] = rc(wire.at[blk(vb, 4), half_a[d]], wire.at[blk(vb, 4), half_a[d]], qdev)

    def ag_begin():
        for cp in (q_b, fa[1, 1], fa[-1, 1], fb_own[1, 1], fb_own[-1, 1], q_a[0]):
            cp.start()

    sent.extend((q_b, fa[1, 1], fa[-1, 1], fb_own[1, 1], fb_own[-1, 1], q_a[0]))

    def ag_a(s):
        for d in (1, -1):
            fa[d, s].wait_recv()
            if s < 4:
                start(fa[d, s + 1])
                start(q_a[-d * s])
            else:
                start(q_a[4, d])

    def ag_b(s, which):
        for d in (1, -1):
            which[d, s].wait_recv()
            if s < 4:
                start(which[d, s + 1])

    def crow(gr, tt):
        return pl.multiple_of(512 * gr + 64 * tt, 32)

    def cblk(gr, yy, off=0, n=64):
        return cot.at[pl.ds(pl.multiple_of(512 * gr + 64 * (2 * yy + c) + off, 32), n)]

    y1, ym1, y2 = (y + 1) % 4, (y + 3) % 4, (y + 2) % 4
    cot_p = {
        o: rc(cot_in.at[pl.ds(o, 32)], cblk(1, y, o, 32), psame) for o in (0, 32)
    }
    own_c = pltpu.make_async_copy(cot_in, cblk(0, y), lsem.at[3])
    cot_y, cot_h, cot_core = {}, {}, {}
    first = {1: 0, -1: 32}
    for gr in (0, 1):
        for d in (1, -1):
            for o in (0, 32):
                mine = cot_in.at[pl.ds(o, 32)] if gr == 0 else cblk(1, y, o, 32)
                cot_y[gr, d, o] = rc(mine, cblk(gr, y, o, 32), ydev[d])
        cot_h[gr, 1] = rc(cblk(gr, ym1, 0, 32), cblk(gr, ym1, 0, 32), ydev[1])
        cot_h[gr, -1] = rc(cblk(gr, y1, 32, 32), cblk(gr, y1, 32, 32), ydev[-1])
        mine = cot_in if gr == 0 else cblk(1, y)
        cot_core[gr, 0] = rc(mine, cblk(gr, y), core)
        cot_core[gr, 1] = rc(cblk(gr, ym1), cblk(gr, ym1), core)
        cot_core[gr, -1] = rc(cblk(gr, y1), cblk(gr, y1), core)
        cot_core[gr, 2] = rc(cblk(gr, y2, 0, 32), cblk(gr, y2, 0, 32), core)
        cot_core[gr, -2] = rc(cblk(gr, y2, 32, 32), cblk(gr, y2, 32, 32), core)

    def cot_begin():
        for o in (0, 1):
            for d in (1, -1):
                start(cot_y[0, d, first[d] if o == 0 else 32 - first[d]])
        start(cot_core[0, 0])

    def cot_partner():
        for o in (0, 32):
            cot_p[o].wait_recv()
        for o in (0, 1):
            for d in (1, -1):
                start(cot_y[1, d, first[d] if o == 0 else 32 - first[d]])
        start(cot_core[1, 0])

    def cot_forward(gr):
        for d in (1, -1):
            cot_y[gr, d, first[d]].wait_recv()
            start(cot_h[gr, d])

    def cot_rest(gr):
        for d in (1, -1):
            cot_y[gr, d, 32 - first[d]].wait_recv()
            start(cot_core[gr, d])

    def cot_last(gr):
        for d in (1, -1):
            cot_h[gr, d].wait_recv()
            start(cot_core[gr, 2 * d])

    def cot_end(gr):
        for k in (0, 1, -1, 2, -2):
            cot_core[gr, k].wait_recv()

    def rows_of(h, b):
        return pl.ds(pl.multiple_of(HALF * h + 400 * b, 16), 400)

    def cols_of(gr):
        return slice(512 * gr, 512 * gr + 512)

    hid_p, hid_core, hid_own = {}, {}, {}
    for h in (0, 1):
        v_to = jnp.where(h == 1 - half, 1 - xb, xb)
        for o in (0, 1):
            b = 1 - v_to if o == 0 else v_to
            hid_p[h, o] = rc(hid.at[rows_of(h, b)], ht.at[rows_of(0, b), cols_of(1)], pcore[h])
    for h in (0, 1):
        whole = hid.at[HALF * h : HALF * h + HALF]
        hid_core[h] = rc(whole, ht.at[:, cols_of(0)], core)
        hid_own[h] = pltpu.make_async_copy(whole, ht.at[:, cols_of(0)], lsem.at[4])

    def hidden_rows(lo, hi):
        @pl.loop(lo, hi)
        def _(i):
            r = pl.ds(pl.multiple_of(32 * i, 32), 32)
            gv = gate[r, :].astype(F32)
            uv = up[r, :].astype(F32)
            hid[r, :] = (gv * jax.nn.sigmoid(gv) * uv).astype(BF)

    def both(fn):
        for h in (0, 1):
            pl.when(c == h)(lambda h=h: fn(h))

    def cot_to_partner():
        for o in (0, 32):
            cot_p[o].start()

    sent.extend(cot_p.values())

    @pl.when(not_r)
    def _():
        swap_w.start()
        cot_to_partner()

    own_c.start()
    cot_begin()

    @pl.when(is_r)
    def _():
        own_w.start()
        own_w.wait()
        ag_begin()

    row = lax.broadcasted_iota(jnp.int32, (TOK, TOK), 0)
    lane = lax.broadcasted_iota(jnp.int32, (TOK, TOK), 1)
    eye[...] = jnp.where(row == lane, 1.0, 0.0).astype(BF)

    load_gate.wait()
    load_up.wait()
    hidden_rows(0, 15)

    pl.when(is_r)(cot_to_partner)

    @pl.when(not_r)
    def _():
        swap_w.wait_recv()
        ag_begin()

    hidden_rows(15, 50)

    @pl.when(not_r)
    def _():
        for o in (0, 1):
            for h in (0, 1):
                hid_p[h, o].start()

    @pl.when(is_r)
    def _():
        both(lambda h: hid_own[h].start())
        both(lambda h: hid_core[1 - h].start())

    def turn(gr):
        hs[512 * gr : 512 * gr + 512, :] = dot_nt(eye[...], ht[:, cols_of(gr)]).astype(BF)

    def wgrad(b):
        left = [[] for _ in range(8)]
        lhs = ht[pl.ds(pl.multiple_of(400 * b, 16), 400), :]
        for n in range(5):
            acc = dot(lhs, cot[:, 512 * n : 512 * n + 512])
            for i in range(8):
                for j in range(4):
                    p = 4 * n + j
                    col = acc[50 * i : 50 * i + 50, 128 * j : 128 * j + 128]
                    g[8 * b + i, 48 * p : 48 * p + 48, :] = col[:48].astype(BF)
                    left[i].append(col[48:50])
        for i in range(8):
            tail = jnp.concatenate(left[i] + [jnp.zeros((8, 128), F32)], axis=0)
            g[8 * b + i, 960:1008, :] = tail.astype(BF)

    def unpack(b):
        tails = [wire[8 * b + i, 960:1008, :].astype(F32) for i in range(8)]
        for p in range(20):
            rows = []
            for i in range(8):
                rows.append(wire[8 * b + i, 48 * p : 48 * p + 48, :].astype(F32))
                rows.append(tails[i][2 * p : 2 * p + 2])
            w[pl.ds(pl.multiple_of(400 * b, 16), 400), 128 * p : 128 * p + 128] = jnp.concatenate(rows, axis=0).astype(BF)

    cut_a, cut_b = slice(0, AG), slice(AG, WR)
    part_b = {1: pl.ds(AG, 272), -1: pl.ds(AG + 272, 256)}

    def kidx(k):
        return k + 3

    ga = {k: rc(g.at[blk(1 - vb, k), cut_a], x_in.at[kidx(k)], qdev) for k in ORDER}
    ha = {1: pl.ds(0, 240), -1: pl.ds(240, 240)}
    hb = {1: pl.ds(0, 272), -1: pl.ds(272, 256)}
    ra_c, rb_c = {}, {}
    for s in (1, 2, 3, 4):
        for d in (1, -1):
            if s == 1:
                ra_c[d, s] = rc(x_in.at[kidx(4), ha[d]], ra.at[(1 - d) // 2, 0, ha[d]], zdev[d])
            else:
                ra_c[d, s] = rc(x_in.at[kidx(d * (5 - s))], ra.at[(1 - d) // 2, s - 1], zdev[d])
            for bb, b in ((0, vb), (1, 1 - vb)):
                if s == 1:
                    rb_c[bb, d, s] = rc(g.at[blk(b, 4), part_b[d]], rb.at[bb, (1 - d) // 2, 0, hb[d]], zdev[d])
                else:
                    rb_c[bb, d, s] = rc(g.at[blk(b, d * (5 - s)), cut_b], rb.at[bb, (1 - d) // 2, s - 1], zdev[d])
    fin_q = rc(fq, fb, qdev)
    swap_ga = rc(stage2.at[cut_a], stage3.at[cut_a], pother)
    swap_gb = rc(stage2.at[cut_b], stage3.at[cut_b], pother)

    def add_into(dst, *terms):
        n = dst.shape[0]
        step = next(v for v in (176, 160, 136, 128, 120, 32, 16) if n % v == 0 and v % 16 == 0)

        @pl.loop(0, n // step)
        def _(i):
            r = pl.ds(pl.multiple_of(i * step, 16), step)
            v = dst[r, :].astype(F32)
            for term in terms:
                v = v + term[r, :].astype(F32)
            dst[r, :] = v.astype(dst.dtype)

    def rs_begin(bb):
        for d in (1, -1):
            start(rb_c[bb, d, 1])
        if bb == 1:
            start(ga[4])

    def rs_x(k):
        ga[k].wait_recv()
        add_into(x_in.at[kidx(k)], g.at[blk(vb, k), cut_a])

    def rs_first():
        rs_x(4)
        for d in (1, -1):
            start(ra_c[d, 1])

    def rs_a(s, d):
        k = d * (5 - s)
        rs_x(k)
        ra_c[d, s - 1].wait_recv()
        rows = ha[d] if s == 2 else pl.ds(0, AG)
        add_into(x_in.at[kidx(k), rows], ra.at[(1 - d) // 2, s - 2, rows])
        start(ra_c[d, s])

    def rs_b(bb, s):
        b = 1 - vb if bb == 1 else vb
        for d in (1, -1):
            k = d * (5 - s)
            rb_c[bb, d, s - 1].wait_recv()
            if s == 2:
                dst, src = g.at[blk(b, k), part_b[d]], rb.at[bb, (1 - d) // 2, 0, hb[d]]
            else:
                dst, src = g.at[blk(b, k), cut_b], rb.at[bb, (1 - d) // 2, s - 2]
            add_into(dst, src)
            start(rb_c[bb, d, s])

    def rs_b_other():
        for d in (1, -1):
            rb_c[1, d, 4].wait_recv()
        fq[...] = (
            g[blk(1 - vb, 0), cut_b, :].astype(F32)
            + rb[1, 0, 3].astype(F32)
            + rb[1, 1, 3].astype(F32)
        ).astype(BF)
        start(fin_q)

    def swap_out(rows, cp, total):
        res[rows, :] = total

        @pl.when(not_r)
        def _():
            stage2[rows, :] = total.astype(BF)
            cp.start()

    def rs_b_end():
        for d in (1, -1):
            rb_c[0, d, 4].wait_recv()
        part = g[blk(vb, 0), cut_b, :].astype(F32) + rb[0, 0, 3].astype(F32) + rb[0, 1, 3].astype(F32)
        fin_q.wait_recv()
        swap_out(cut_b, swap_gb, part + fb[...].astype(F32))

    def rs_a_end():
        for d in (1, -1):
            ra_c[d, 4].wait_recv()
        total = x_in[kidx(0)].astype(F32) + ra[0, 3].astype(F32) + ra[1, 3].astype(F32)
        swap_out(cut_a, swap_ga, total)

    def rs_end():
        @pl.when(not_r)
        def _():
            swap_gb.wait_recv()
            res[cut_b, :] = stage3[cut_b, :].astype(F32)
            swap_ga.wait_recv()
            res[cut_a, :] = stage3[cut_a, :].astype(F32)
            swap_ga.wait_send()
            swap_gb.wait_send()

    def layer(gr, ch):
        @pl.loop(0, 5)
        def _(n):
            off = pl.multiple_of(256 * n, 256)
            acc = dot(hs[512 * gr : 512 * gr + 512, :], w[:, pl.ds(pl.multiple_of(1280 * ch + off, 256), 256)])
            for tt in range(8):
                r = 64 * (tt // 2)
                lp[gr, ch, tt % 2, r : r + 64, pl.ds(off, 256)] = acc[64 * tt : 64 * tt + 64].astype(BF)

    l_core, l_y1, l_y2, l_p = {}, {}, {}, {}

    def yrow(yy, off=0, n=64):
        return pl.ds(pl.multiple_of(64 * yy + off, 32), n)

    for gr in (1, 0):
        for ch in (0, 1):
            l_core[gr, ch] = rc(lp.at[gr, ch, 1 - c], lc.at[gr, ch], core)
            for d in (1, -1):
                o = 0 if d == 1 else 32
                l_y1[gr, ch, d] = rc(lc.at[gr, ch, yrow(y2, o, 32)], ly.at[gr, ch, (1 - d) // 2], ydev[d])
                to = y1 if d == 1 else ym1
                l_y2[gr, ch, d] = rc(lc.at[gr, ch, yrow(to)], lf.at[gr, ch, (1 - d) // 2], ydev[d])
    for ch in (0, 1):
        l_p[ch] = rc(lz.at[ch], lq.at[ch], psame)

    def layer_core(gr, ch):
        l_core[gr, ch].wait_recv()
        add_into(lc.at[gr, ch], lp.at[gr, ch, c])
        for d in (1, -1):
            start(l_y1[gr, ch, d])

    def layer_y(gr, ch):
        for d in (1, -1):
            l_y1[gr, ch, d].wait_recv()
            o = 0 if d == 1 else 32
            to = y1 if d == 1 else ym1
            add_into(lc.at[gr, ch, yrow(to, o, 32)], ly.at[gr, ch, (1 - d) // 2])
            start(l_y2[gr, ch, d])

    def layer_end(gr, ch):
        for d in (1, -1):
            l_y2[gr, ch, d].wait_recv()
        total = lc[gr, ch, yrow(y), :].astype(F32) + lf[gr, ch, 0].astype(F32) + lf[gr, ch, 1].astype(F32)
        if gr == 1:
            lz[ch] = total.astype(BF)
            start(l_p[ch])
        else:
            l_p[ch].wait_recv()
            out_ref[:, 1280 * ch : 1280 * ch + 1280] = (total + lq[ch].astype(F32)).astype(BF)

    def drows(h, q):
        return pl.ds(HALF * h + 400 * q, 400)

    d_p, d_core, d_own = {}, {}, {}
    for h in (0, 1):
        for q in (0, 1):
            src = dd.at[1, 400 * q : 400 * q + 400]
            d_p["same", h, q] = rc(src, dr.at[drows(h, q)], psame)
            d_p["other", h, q] = rc(src, dr.at[drows(h, q)], pother)
            src = dd.at[0, 400 * q : 400 * q + 400]
            d_core[h, q] = rc(src, dr.at[drows(h, q)], core)
            d_own[h, q] = pltpu.make_async_copy(src, dr.at[drows(h, q)], lsem.at[5 + q])

    def dhidden(gr, q):
        dd[gr, 400 * q : 400 * q + 400, :] = dot_nt(
            w[400 * q : 400 * q + 400, :], cot[512 * gr : 512 * gr + 512, :]
        ).astype(BF)

    def d_send_p(q):
        @pl.when(is_r)
        def _():
            both(lambda h: d_p["same", h, q].start())

        @pl.when(not_r)
        def _():
            both(lambda h: d_p["other", h, q].start())

    def d_send_core(q):
        @pl.when(is_r)
        def _():
            both(lambda h: d_own[h, q].start())

        @pl.when(not_r)
        def _():
            both(lambda h: d_core[h, q].start())

    def d_recv(q):
        @pl.when(is_r)
        def _():
            both(lambda h: d_own[h, q].wait())
            both(lambda h: d_core[1 - h, q].wait_recv())

        @pl.when(not_r)
        def _():
            def arrive(h):
                d_p["same", h, q].wait_recv()
                d_p["other", 1 - h, q].wait_recv()

            both(arrive)

    def d_sent():
        for q in (0, 1):
            @pl.when(is_r)
            def _():
                both(lambda h: d_p["same", h, q].wait_send())

            @pl.when(not_r)
            def _():
                both(lambda h: d_p["other", h, q].wait_send())
                both(lambda h: d_core[h, q].wait_send())

    q_b.wait_recv()
    for d in (1, -1):
        start(fb_q[d, 1])
    ag_a(1)
    cot_forward(0)

    @pl.when(is_r)
    def _():
        both(lambda h: hid_own[h].wait())

    @pl.when(not_r)
    def _():
        both(lambda h: hid_core[h].wait_recv())

    turn(0)
    ag_b(1, fb_own)
    cot_partner()
    ag_b(1, fb_q)
    cot_rest(0)
    cot_last(0)
    ag_a(2)
    cot_forward(1)
    ag_b(2, fb_own)
    ag_b(2, fb_q)
    cot_rest(1)
    ag_a(3)
    cot_last(1)
    ag_b(3, fb_own)
    cot_end(0)
    cot_end(1)
    own_c.wait()
    both(lambda h: hid_p[h, 0].wait_recv())
    wgrad(1 - vb)
    rs_begin(1)
    ag_b(3, fb_q)
    ag_a(4)
    for k in ORDER[1:]:
        start(ga[k])
    both(lambda h: hid_p[h, 1].wait_recv())
    wgrad(vb)
    rs_begin(0)
    ag_b(4, fb_own)
    ag_b(4, fb_q)
    rs_b(1, 2)
    turn(1)
    rs_first()
    for k in (0, 1, -1, 2, -2, 3, -3):
        q_a[k].wait_recv()
    for d in (1, -1):
        q_a[4, d].wait_recv()
    unpack(0)
    unpack(1)
    layer(1, 0)
    start(l_core[1, 0])
    rs_b(0, 2)
    dhidden(1, 0)
    d_send_p(0)
    layer_core(1, 0)
    rs_a(2, 1)
    dhidden(1, 1)
    d_send_p(1)
    rs_b(1, 3)
    rs_a(2, -1)
    layer(1, 1)
    start(l_core[1, 1])
    rs_b(0, 3)
    layer_y(1, 0)
    dhidden(0, 0)
    d_send_core(0)
    rs_a(3, 1)
    layer_core(1, 1)
    rs_b(1, 4)
    rs_a(3, -1)
    dhidden(0, 1)
    d_send_core(1)
    layer(0, 0)
    start(l_core[0, 0])
    rs_b(0, 4)
    layer_y(1, 1)
    rs_a(4, 1)
    layer(0, 1)
    start(l_core[0, 1])
    layer_core(0, 0)
    rs_a(4, -1)
    layer_end(1, 0)
    rs_b_other()
    layer_core(0, 1)
    layer_y(0, 0)
    layer_end(1, 1)
    rs_x(0)
    layer_y(0, 1)
    rs_b_end()
    rs_a_end()
    d_recv(0)
    d_recv(1)
    layer_end(0, 0)
    layer_end(0, 1)
    rs_end()

    for cp in sent:
        cp.wait_send()

    @pl.when(not_r)
    def _():
        swap_w.wait_send()
        for o in (0, 1):
            for h in (0, 1):
                hid_p[h, o].wait_send()

    @pl.when(is_r)
    def _():
        both(lambda h: hid_core[1 - h].wait_send())

    d_sent()


def last_kernel(dr, gate, up, out_in, res, gg_ref, ug_ref, out_ref, wg_ref):
    dv = dr[...].astype(F32)
    gv = gate[...].astype(F32)
    uv = up[...].astype(F32)
    sv = jax.nn.sigmoid(gv)
    gg_ref[...] = (dv * uv * sv * (1.0 + gv * (1.0 - sv))).astype(BF)
    ug_ref[...] = (dv * (gv * sv)).astype(BF)

    @pl.when(pl.program_id(0) == 0)
    def _():
        out_ref[...] = out_in[...]
        for p in range(20):
            cols = slice(128 * p, 128 * p + 128)
            wg_ref[0:48, cols] = res[48 * p : 48 * p + 48, :] * SCALE
            wg_ref[48:50, cols] = res[960 + 2 * p : 962 + 2 * p, :] * SCALE


def body(gate_pre, up_pre, down_codes, down_scales, cotangent):
    vmem = pl.BlockSpec(memory_space=pltpu.VMEM)
    anywhere = pl.BlockSpec(memory_space=pl.ANY)
    gate_t, up_t = gate_pre.T, up_pre.T
    out, dhid, total = pl.pallas_call(
        kernel,
        out_shape=(
            jax.ShapeDtypeStruct((64, D), BF),
            jax.ShapeDtypeStruct((UNITS, TOK), BF),
            jax.ShapeDtypeStruct((WR, 128), F32),
        ),
        in_specs=[anywhere, anywhere, vmem, vmem, vmem],
        out_specs=(vmem, vmem, vmem),
        scratch_shapes=[
            pltpu.VMEM((UNITS, TOK), BF),
            pltpu.VMEM((UNITS, TOK), BF),
            pltpu.VMEM((16, WR, 128), BF),
            pltpu.VMEM((WR, 128), BF),
            pltpu.VMEM((HALF, D), BF),
            pltpu.VMEM((1024, D), BF),
            pltpu.VMEM((UNITS, TOK), BF),
            pltpu.VMEM((HALF, 1024), BF),
            pltpu.VMEM((1024, HALF), BF),
            pltpu.VMEM((TOK, TOK), BF),
            pltpu.VMEM((16, WR, 128), BF),
            pltpu.VMEM((8, AG, 128), BF),
            pltpu.VMEM((2, 4, AG, 128), BF),
            pltpu.VMEM((2, 2, 4, BG, 128), BF),
            pltpu.VMEM((BG, 128), BF),
            pltpu.VMEM((BG, 128), BF),
            pltpu.VMEM((WR, 128), BF),
            pltpu.VMEM((WR, 128), BF),
            pltpu.VMEM((2, 2, 2, 256, 1280), BF),
            pltpu.VMEM((2, 2, 256, 1280), BF),
            pltpu.VMEM((2, 2, 2, 32, 1280), BF),
            pltpu.VMEM((2, 2, 2, 64, 1280), BF),
            pltpu.VMEM((2, 64, 1280), BF),
            pltpu.VMEM((2, 64, 1280), BF),
            pltpu.VMEM((2, HALF, TOK), BF),
            pltpu.SemaphoreType.DMA((NSEM,)),
            pltpu.SemaphoreType.DMA((NSEM,)),
            pltpu.SemaphoreType.DMA((8,)),
        ],
        compiler_params=pltpu.CompilerParams(
            collective_id=0, has_side_effects=True, vmem_limit_bytes=62 << 20
        ),
        cost_estimate=pl.CostEstimate(flops=25_000_000_000, bytes_accessed=10_000_000, transcendentals=2_000_000),
    )(gate_t, up_t, down_codes, down_scales, cotangent)

    def whole(rows, cols):
        return pl.BlockSpec((rows, cols), lambda i: (0, 0))

    part = pl.BlockSpec((320, TOK), lambda i: (i, 0))
    gate_grad, up_grad, layer_out, weight_grad = pl.pallas_call(
        last_kernel,
        grid=(5,),
        out_shape=(
            jax.ShapeDtypeStruct((UNITS, TOK), BF),
            jax.ShapeDtypeStruct((UNITS, TOK), BF),
            jax.ShapeDtypeStruct((64, D), BF),
            jax.ShapeDtypeStruct((50, D), F32),
        ),
        in_specs=[part, part, part, whole(64, D), whole(WR, 128)],
        out_specs=(part, part, whole(64, D), whole(50, D)),
        compiler_params=pltpu.CompilerParams(vmem_limit_bytes=62 << 20),
        cost_estimate=pl.CostEstimate(flops=20_000_000, bytes_accessed=10_000_000, transcendentals=1_000_000),
    )(dhid, gate_t, up_t, out, total)
    return layer_out, gate_grad.T, up_grad.T, weight_grad


def solution(mesh):
    return jax.shard_map(
        body,
        mesh=mesh,
        in_specs=(
            P("dp", "tensor"),
            P("dp", "tensor"),
            P(("tensor", "dp"), None),
            P(("tensor", "dp"), None),
            P(("dp", "tensor"), None),
        ),
        out_specs=(
            P(("dp", "tensor"), None),
            P("dp", "tensor"),
            P("dp", "tensor"),
            P(("tensor", "dp"), None),
        ),
        check_vma=False,
    )
```

time: 122 us -> 99.1 us (0.81)
  local copies, waits for them, and re-layouts: 15.1 us -> 1.4 us
  Pallas kernels: 106 us -> 96.7 us
    pallas_call x1, Pallas kernels: 106 us -> 89.5 us  [body(): pl.pallas_call(kernel, out_shape=(jax.ShapeDtypeStruct((64, D), BF), jax....]
    unnamed x13 -> x1, local copies, waits for them, and re-layouts: 9.08 us -> 1.4 us
    pallas_call x0 -> x1, Pallas kernels: none -> 7.12 us  [body(): pl.pallas_call(last_kernel, grid=(5,), out_shape=(jax.ShapeDtypeStruct((U...]
    pallas_call x2 -> x0, local copies, waits for them, and re-layouts: 5.98 us -> none  [body(): pl.pallas_call(kernel, out_shape=(jax.ShapeDtypeStruct((64, D), BF), jax....]
where the time goes in v2:
time: 99.1 us; the launch traced here: 98.9 us
  Pallas kernels  96.7 us (98%)
  local copies, waits for them, and re-layouts  1.4 us (1%)
    pallas_call x1, Pallas kernels, body(): pl.pallas_call(kernel, out_shape=(jax.ShapeDtypeStruct((64, D), BF), jax....  89.5 us
    pallas_call x1, Pallas kernels, body(): pl.pallas_call(last_kernel, grid=(5,), out_shape=(jax.ShapeDtypeStruct((U...  7.12 us

profile of v2, /device:TPU:1, one launch (start us, length us, event | category | flops | bytes accessed | tf_op | source)
XLA Modules:
  0.0 98.9 jit_solution(7549810897132876887)
XLA Ops:
  0.6 1.4 %copy.9.scales_ref = f32[50,10]{1,0:T(8,128)} copy(f32[50,10]{0,1:T(8,128)} %param.8) | data formatting | bytes 4000 | tf_op args[3]
  2.0 89.5 %shard_map.84 = (bf16[64,2560]{1,0:T(8,128)(2,1)}, bf16[1600,512]{1,0:T(8,128)(2,1)}, f32[1008,128]{1,0:T(8,128)}) custom-call(bf16[1600,512]{1,0:T(8,128)(2,1)} %bitcast.4, bf16[1600,512]{1,0:T(8,128)(2,1)} %bitcast.6, bf16[50,2560]{1,0:T(8,128)(2,1)} %codes_ref.1, f32[50,10]{1,0:T(8,128)} %copy.9.scales_ref, bf16[64,2560]{1,0:T(8,128)(2,1)} %cot_in.1), custom_call_target="tpu_custom_call" | custom-call | flops 24999999488 | bytes 10000000 | tf_op jit(solution)/shard_map/pallas_call | solution.py:670
  91.6 7.1 %shard_map.85 = (bf16[1600,512]{1,0:T(8,128)(2,1)}, bf16[1600,512]{1,0:T(8,128)(2,1)}, bf16[64,2560]{1,0:T(8,128)(2,1)}, f32[50,2560]{1,0:T(8,128)}) custom-call(bf16[1600,512]{1,0:T(8,128)(2,1)} %get-tuple-element.11.dr, bf16[1600,512]{1,0:T(8,128)(2,1)} %bitcast.5, bf16[1600,512]{1,0:T(8,128)(2,1)} %bitcast.7, bf16[64,2560]{1,0:T(8,128)(2,1)} %get-tuple-element.12.out_in, ...), custom_call_target="tpu_custom_call" | custom-call | flops 20000000 | bytes 10000000 | tf_op jit(solution)/shard_map/pallas_call | solution.py:719

commit v3 on v2

--- a/solution.py
+++ b/solution.py
@@ -16,6 +16,8 @@
 AR, BR = 576, 432
 AG, BG = 480, 528
 NSEM = 160
+LIMIT = 400 << 17
+PART = 160
 SCALE = float(16384) ** -0.5
 ORDER = (4, 3, -3, 2, -2, 1, -1, 0)
 
@@ -29,9 +31,9 @@
 
 
 def kernel(
-    gate_hbm, up_hbm, codes_ref, scales_ref, cot_in,
+    gate_hbm, up_hbm, codes_hbm, scales_ref, cot_hbm,
     out_ref, dr, res,
-    gate, up, wire, stage, w, cot, hid, ht, hs, eye, g, x_in, ra, rb, fq, fb, stage2, stage3,
+    gate, up, codes_ref, cot_in, wire, stage, w, cot, hid, ht, hs, eye, g, x_in, ra, rb, fq, fb, stage2, stage3,
     lp, lc, ly, lf, lz, lq, dd, ssem, rsem, lsem,
 ):
     dp, t = lax.axis_index("dp"), lax.axis_index("tensor")
@@ -51,14 +53,17 @@
     pcore = ((pdp, 2 * y), (pdp, 2 * y + 1))
 
     count = [0]
+    index = {}
 
     def rc(src, dst, dev):
         i = count[0]
         count[0] += 1
-        return pltpu.make_async_remote_copy(
+        cp = pltpu.make_async_remote_copy(
             src_ref=src, dst_ref=dst, send_sem=ssem.at[i], recv_sem=rsem.at[i],
             device_id=dev, device_id_type=MESH,
         )
+        index[id(cp)] = i
+        return cp
 
     sent = []
 
@@ -68,6 +73,10 @@
 
     load_gate = pltpu.make_async_copy(gate_hbm, gate, lsem.at[0])
     load_up = pltpu.make_async_copy(up_hbm, up, lsem.at[1])
+    load_codes = pltpu.make_async_copy(codes_hbm, codes_ref, lsem.at[7])
+    load_cot = pltpu.make_async_copy(cot_hbm, cot_in, lsem.at[8])
+    load_codes.start()
+    load_cot.start()
     load_gate.start()
     load_up.start()
 
@@ -77,14 +86,17 @@
         pl.semaphore_signal(barrier, inc=1, device_id=dev, device_id_type=MESH)
 
     left = []
+    scales = scales_ref[...].T
+    load_codes.wait()
     for p in range(20):
-        scale = scales_ref[:, p // 2 : p // 2 + 1]
+        scale = scales[:, p // 2 : p // 2 + 1]
         piece = codes_ref[:, 128 * p : 128 * p + 128].astype(F32) * scale
         stage[48 * p : 48 * p + 48, :] = piece[:48].astype(BF)
         left.append(piece[48:50])
     left.append(jnp.zeros((8, 128), F32))
     stage[960:1008, :] = jnp.concatenate(left, axis=0).astype(BF)
 
+    load_cot.wait()
     pl.semaphore_wait(barrier, len(everyone))
 
     def blk(b, k):
@@ -96,7 +108,7 @@
     half_b = {1: pl.ds(AR, 224), -1: pl.ds(AR + 224, 208)}
     own_slot = 8 * vb + z
 
-    swap_w = rc(stage, wire.at[8 * xb + z], pother)
+    swap_w = [rc(stage.at[rows], wire.at[8 * xb + z, rows], pother) for rows in (rows_b, rows_a)]
     own_w = pltpu.make_async_copy(stage, wire.at[own_slot], lsem.at[2])
 
     def ring(b, rows, halves):
@@ -121,9 +133,15 @@
     for d in (1, -1):
         q_a[4, d] = rc(wire.at[blk(vb, 4), half_a[d]], wire.at[blk(vb, 4), half_a[d]], qdev)
 
-    def ag_begin():
-        for cp in (q_b, fa[1, 1], fa[-1, 1], fb_own[1, 1], fb_own[-1, 1], q_a[0]):
-            cp.start()
+    begin_b = (q_b, fb_own[1, 1], fb_own[-1, 1])
+    begin_a = (fa[1, 1], fa[-1, 1], q_a[0])
+
+    def from_stage(cp, rows, dev):
+        i = index[id(cp)]
+        pltpu.make_async_remote_copy(
+            src_ref=stage.at[rows], dst_ref=wire.at[own_slot, rows], send_sem=ssem.at[i], recv_sem=rsem.at[i],
+            device_id=dev, device_id_type=MESH,
+        ).start()
 
     sent.extend((q_b, fa[1, 1], fa[-1, 1], fb_own[1, 1], fb_own[-1, 1], q_a[0]))
 
@@ -239,7 +257,8 @@
 
     @pl.when(not_r)
     def _():
-        swap_w.start()
+        for cp in swap_w:
+            cp.start()
         cot_to_partner()
 
     own_c.start()
@@ -247,9 +266,13 @@
 
     @pl.when(is_r)
     def _():
+        from_stage(q_b, rows_b, qdev)
+        for d in (1, -1):
+            from_stage(fa[d, 1], rows_a, zdev[d])
+        for d in (1, -1):
+            from_stage(fb_own[d, 1], rows_b, zdev[d])
+        from_stage(q_a[0], rows_a, qdev)
         own_w.start()
-        own_w.wait()
-        ag_begin()
 
     row = lax.broadcasted_iota(jnp.int32, (TOK, TOK), 0)
     lane = lax.broadcasted_iota(jnp.int32, (TOK, TOK), 1)
@@ -263,8 +286,10 @@
 
     @pl.when(not_r)
     def _():
-        swap_w.wait_recv()
-        ag_begin()
+        for cp, begin in zip(swap_w, (begin_b, begin_a)):
+            cp.wait_recv()
+            for follow in begin:
+                follow.start()
 
     hidden_rows(15, 50)
 
@@ -469,23 +494,28 @@
             l_p[ch].wait_recv()
             out_ref[:, 1280 * ch : 1280 * ch + 1280] = (total + lq[ch].astype(F32)).astype(BF)
 
-    def drows(h, q):
-        return pl.ds(HALF * h + 400 * q, 400)
+    def half_of(o):
+        return vb if o == 0 else 1 - vb
+
+    def rows_at(q):
+        return pl.ds(pl.multiple_of(400 * q, 16), 400)
+
+    def drows(h, o):
+        return pl.ds(pl.multiple_of(HALF * h + 400 * half_of(o), 16), 400)
 
     d_p, d_core, d_own = {}, {}, {}
     for h in (0, 1):
         for q in (0, 1):
-            src = dd.at[1, 400 * q : 400 * q + 400]
+            src = dd.at[1, rows_at(half_of(q))]
             d_p["same", h, q] = rc(src, dr.at[drows(h, q)], psame)
             d_p["other", h, q] = rc(src, dr.at[drows(h, q)], pother)
-            src = dd.at[0, 400 * q : 400 * q + 400]
+            src = dd.at[0, rows_at(half_of(q))]
             d_core[h, q] = rc(src, dr.at[drows(h, q)], core)
             d_own[h, q] = pltpu.make_async_copy(src, dr.at[drows(h, q)], lsem.at[5 + q])
 
-    def dhidden(gr, q):
-        dd[gr, 400 * q : 400 * q + 400, :] = dot_nt(
-            w[400 * q : 400 * q + 400, :], cot[512 * gr : 512 * gr + 512, :]
-        ).astype(BF)
+    def dhidden(gr, o):
+        r = rows_at(half_of(o))
+        dd[gr, r, :] = dot_nt(w[r, :], cot[512 * gr : 512 * gr + 512, :]).astype(BF)
 
     def d_send_p(q):
         @pl.when(is_r)
@@ -539,6 +569,7 @@
     @pl.when(is_r)
     def _():
         both(lambda h: hid_own[h].wait())
+        own_w.wait()
 
     @pl.when(not_r)
     def _():
@@ -564,29 +595,29 @@
     both(lambda h: hid_p[h, 0].wait_recv())
     wgrad(1 - vb)
     rs_begin(1)
+    ag_a(4)
     ag_b(3, fb_q)
-    ag_a(4)
     for k in ORDER[1:]:
         start(ga[k])
     both(lambda h: hid_p[h, 1].wait_recv())
     wgrad(vb)
     rs_begin(0)
     ag_b(4, fb_own)
+    unpack(vb)
+    dhidden(1, 0)
+    d_send_p(0)
+    rs_b(1, 2)
     ag_b(4, fb_q)
-    rs_b(1, 2)
+    rs_first()
     turn(1)
-    rs_first()
     for k in (0, 1, -1, 2, -2, 3, -3):
         q_a[k].wait_recv()
     for d in (1, -1):
         q_a[4, d].wait_recv()
-    unpack(0)
-    unpack(1)
+    unpack(1 - vb)
     layer(1, 0)
     start(l_core[1, 0])
     rs_b(0, 2)
-    dhidden(1, 0)
-    d_send_p(0)
     layer_core(1, 0)
     rs_a(2, 1)
     dhidden(1, 1)
@@ -621,10 +652,10 @@
     layer_end(1, 1)
     rs_x(0)
     layer_y(0, 1)
+    for q in (0, 1):
+        d_recv(q)
     rs_b_end()
     rs_a_end()
-    d_recv(0)
-    d_recv(1)
     layer_end(0, 0)
     layer_end(0, 1)
     rs_end()
@@ -634,7 +665,8 @@
 
     @pl.when(not_r)
     def _():
-        swap_w.wait_send()
+        for cp in swap_w:
+            cp.wait_send()
         for o in (0, 1):
             for h in (0, 1):
                 hid_p[h, o].wait_send()
@@ -646,21 +678,36 @@
     d_sent()
 
 
-def last_kernel(dr, gate, up, out_in, res, gg_ref, ug_ref, out_ref, wg_ref):
-    dv = dr[...].astype(F32)
-    gv = gate[...].astype(F32)
-    uv = up[...].astype(F32)
-    sv = jax.nn.sigmoid(gv)
-    gg_ref[...] = (dv * uv * sv * (1.0 + gv * (1.0 - sv))).astype(BF)
-    ug_ref[...] = (dv * (gv * sv)).astype(BF)
-
-    @pl.when(pl.program_id(0) == 0)
-    def _():
-        out_ref[...] = out_in[...]
-        for p in range(20):
-            cols = slice(128 * p, 128 * p + 128)
-            wg_ref[0:48, cols] = res[48 * p : 48 * p + 48, :] * SCALE
-            wg_ref[48:50, cols] = res[960 + 2 * p : 962 + 2 * p, :] * SCALE
+def last_kernel(dr, gate, up, out, res, gg_hbm, ug_hbm, lo_hbm, wg_hbm, gg, ug, wg, osem):
+    def part(i):
+        return pl.ds(PART * i, PART)
+
+    n = UNITS // PART
+    saves = [pltpu.make_async_copy(out, lo_hbm, osem.at[2 * n])]
+    saves[0].start()
+    for p in range(20):
+        cols = slice(128 * p, 128 * p + 128)
+        wg[0:48, cols] = res[48 * p : 48 * p + 48, :] * SCALE
+        wg[48:50, cols] = res[960 + 2 * p : 962 + 2 * p, :] * SCALE
+    saves.append(pltpu.make_async_copy(wg, wg_hbm, osem.at[2 * n + 1]))
+    saves[1].start()
+    for i in range(n):
+        @pl.loop(0, PART // 16)
+        def _(k):
+            r = pl.ds(pl.multiple_of(PART * i + 16 * k, 16), 16)
+            dv = dr[r, :].astype(F32)
+            gv = gate[r, :].astype(F32)
+            uv = up[r, :].astype(F32)
+            sv = jax.nn.sigmoid(gv)
+            gg[r, :] = (dv * uv * sv * (1.0 + gv * (1.0 - sv))).astype(BF)
+            ug[r, :] = (dv * (gv * sv)).astype(BF)
+
+        for j, (src, dst) in enumerate(((gg, gg_hbm), (ug, ug_hbm))):
+            cp = pltpu.make_async_copy(src.at[part(i)], dst.at[part(i)], osem.at[2 * i + j])
+            cp.start()
+            saves.append(cp)
+    for cp in saves:
+        cp.wait()
 
 
 def body(gate_pre, up_pre, down_codes, down_scales, cotangent):
@@ -674,11 +721,13 @@
             jax.ShapeDtypeStruct((UNITS, TOK), BF),
             jax.ShapeDtypeStruct((WR, 128), F32),
         ),
-        in_specs=[anywhere, anywhere, vmem, vmem, vmem],
-        out_specs=(vmem, vmem, vmem),
+        in_specs=[anywhere, anywhere, anywhere, vmem, anywhere],
+        out_specs=(vmem,) * 3,
         scratch_shapes=[
             pltpu.VMEM((UNITS, TOK), BF),
             pltpu.VMEM((UNITS, TOK), BF),
+            pltpu.VMEM((50, D), BF),
+            pltpu.VMEM((64, D), BF),
             pltpu.VMEM((16, WR, 128), BF),
             pltpu.VMEM((WR, 128), BF),
             pltpu.VMEM((HALF, D), BF),
@@ -704,30 +753,31 @@
             pltpu.VMEM((2, HALF, TOK), BF),
             pltpu.SemaphoreType.DMA((NSEM,)),
             pltpu.SemaphoreType.DMA((NSEM,)),
-            pltpu.SemaphoreType.DMA((8,)),
+            pltpu.SemaphoreType.DMA((16,)),
         ],
         compiler_params=pltpu.CompilerParams(
-            collective_id=0, has_side_effects=True, vmem_limit_bytes=62 << 20
+            collective_id=0, has_side_effects=True, vmem_limit_bytes=LIMIT
         ),
         cost_estimate=pl.CostEstimate(flops=25_000_000_000, bytes_accessed=10_000_000, transcendentals=2_000_000),
-    )(gate_t, up_t, down_codes, down_scales, cotangent)
-
-    def whole(rows, cols):
-        return pl.BlockSpec((rows, cols), lambda i: (0, 0))
-
-    part = pl.BlockSpec((320, TOK), lambda i: (i, 0))
+    )(gate_t, up_t, down_codes, down_scales.T, cotangent)
+
     gate_grad, up_grad, layer_out, weight_grad = pl.pallas_call(
         last_kernel,
-        grid=(5,),
         out_shape=(
             jax.ShapeDtypeStruct((UNITS, TOK), BF),
             jax.ShapeDtypeStruct((UNITS, TOK), BF),
             jax.ShapeDtypeStruct((64, D), BF),
             jax.ShapeDtypeStruct((50, D), F32),
         ),
-        in_specs=[part, part, part, whole(64, D), whole(WR, 128)],
-        out_specs=(part, part, whole(64, D), whole(50, D)),
-        compiler_params=pltpu.CompilerParams(vmem_limit_bytes=62 << 20),
+        in_specs=[vmem] * 5,
+        out_specs=(anywhere,) * 4,
+        scratch_shapes=[
+            pltpu.VMEM((UNITS, TOK), BF),
+            pltpu.VMEM((UNITS, TOK), BF),
+            pltpu.VMEM((50, D), F32),
+            pltpu.SemaphoreType.DMA((2 * UNITS // PART + 2,)),
+        ],
+        compiler_params=pltpu.CompilerParams(vmem_limit_bytes=24 << 20),
         cost_estimate=pl.CostEstimate(flops=20_000_000, bytes_accessed=10_000_000, transcendentals=1_000_000),
     )(dhid, gate_t, up_t, out, total)
     return layer_out, gate_grad.T, up_grad.T, weight_grad

time: 99.1 us -> 92.5 us (0.933)
  Pallas kernels: 96.7 us -> 88.8 us
  local copies, waits for them, and re-layouts: 1.4 us -> 2.63 us
    pallas_call x1, Pallas kernels: 7.12 us -> 3.17 us  [body(): pl.pallas_call(last_kernel, out_shape=(jax.ShapeDtypeStruct((UNITS, TOK),...]
    pallas_call x1, Pallas kernels: 89.5 us -> 85.7 us  [body(): pl.pallas_call(kernel, out_shape=(jax.ShapeDtypeStruct((64, D), BF), jax....]
    unnamed x1 -> x10, local copies, waits for them, and re-layouts: 1.4 us -> 2.63 us
where the time goes in v3:
time: 92.5 us; the launch traced here: 92.3 us
  Pallas kernels  88.8 us (96%)
  local copies, waits for them, and re-layouts  2.63 us (3%)
    pallas_call x1, Pallas kernels, body(): pl.pallas_call(kernel, out_shape=(jax.ShapeDtypeStruct((64, D), BF), jax....  85.7 us
    pallas_call x1, Pallas kernels, body(): pl.pallas_call(last_kernel, out_shape=(jax.ShapeDtypeStruct((UNITS, TOK),...  3.17 us
    unnamed x10, local copies, waits for them, and re-layouts  2.63 us

profile of v3, /device:TPU:1, one launch (start us, length us, event | category | flops | bytes accessed | tf_op | source)
XLA Modules:
  0.0 92.3 jit_solution(4918886948214789791)
XLA Ops:
  0.6 0.0 copy-start.2
  0.6 1.0 %copy-done.2 = bf16[64,2560]{1,0:T(8,128)(2,1)S(1)} copy-done((bf16[64,2560]{1,0:T(8,128)(2,1)S(1)}, bf16[64,2560]{1,0:T(8,128)(2,1)}, u32[]{:S(2)}) %copy-start.2) | copy-done | bytes 327704
  1.6 0.0 copy-start.3
  1.6 1.0 %copy-done.3 = bf16[50,2560]{1,0:T(8,128)(2,1)S(1)} copy-done((bf16[50,2560]{1,0:T(8,128)(2,1)S(1)}, bf16[50,2560]{1,0:T(8,128)(2,1)}, u32[]{:S(2)}) %copy-start.3) | copy-done | bytes 256024
  2.6 0.0 copy-start.4
  2.6 0.7 copy-done.4
  3.3 0.0 copy-start
  3.3 0.0 copy-start.1
  3.3 85.7 %shard_map.84 = (bf16[64,2560]{1,0:T(8,128)(2,1)S(1)}, bf16[1600,512]{1,0:T(8,128)(2,1)S(1)}, f32[1008,128]{1,0:T(8,128)S(1)}) custom-call(bf16[1600,512]{1,0:T(8,128)(2,1)} %bitcast.5, bf16[1600,512]{1,0:T(8,128)(2,1)} %bitcast.7, bf16[50,2560]{1,0:T(8,128)(2,1)S(1)} %copy-done.3, f32[10,50]{1,0:T(8,128)S(1)} %bitcast.9, bf16[64,2560]{1,0:T(8,128)(2,1)S(1)} %copy-done.2), custom_call_target="tpu_custom_call" | custom-call | flops 24999999488 | bytes 10000000 | tf_op jit(solution)/shard_map/pallas_call | solution.py:717
  88.9 0.0 copy-done
  88.9 0.0 copy-done.1
  88.9 3.2 %shard_map.85 = (bf16[1600,512]{1,0:T(8,128)(2,1)}, bf16[1600,512]{1,0:T(8,128)(2,1)}, bf16[64,2560]{1,0:T(8,128)(2,1)}, f32[50,2560]{1,0:T(8,128)}) custom-call(bf16[1600,512]{1,0:T(8,128)(2,1)S(1)} %get-tuple-element.11.dr, bf16[1600,512]{1,0:T(8,128)(2,1)S(1)} %bitcast.6, bf16[1600,512]{1,0:T(8,128)(2,1)S(1)} %bitcast.8, ...), custom_call_target="tpu_custom_call" | custom-call | flops 20000000 | bytes 10000000 | tf_op jit(solution)/shard_map/pallas_call | solution.py:764
Async XLA Ops:
  0.6 1.0 %copy-start.2 = (bf16[64,2560]{1,0:T(8,128)(2,1)S(1)}, bf16[64,2560]{1,0:T(8,128)(2,1)}, u32[]{:S(2)}) copy-start(bf16[64,2560]{1,0:T(8,128)(2,1)} %cot_hbm.1) | copy-start | bytes 983044
  1.6 1.0 %copy-start.3 = (bf16[50,2560]{1,0:T(8,128)(2,1)S(1)}, bf16[50,2560]{1,0:T(8,128)(2,1)}, u32[]{:S(2)}) copy-start(bf16[50,2560]{1,0:T(8,128)(2,1)} %codes_hbm.1) | copy-start | bytes 768004
  2.6 0.7 copy-start.4
  3.3 85.7 %copy-start = (bf16[512,1600]{0,1:T(8,128)(2,1)S(1)}, bf16[512,1600]{0,1:T(8,128)(2,1)}, u32[]{:S(2)}) copy-start(bf16[512,1600]{0,1:T(8,128)(2,1)} %param.5) | copy-start | bytes 4915204
  3.3 85.7 %copy-start.1 = (bf16[512,1600]{0,1:T(8,128)(2,1)S(1)}, bf16[512,1600]{0,1:T(8,128)(2,1)}, u32[]{:S(2)}) copy-start(bf16[512,1600]{0,1:T(8,128)(2,1)} %param.6) | copy-start | bytes 4915204

commit v4 on v3

--- a/solution.py
+++ b/solution.py
@@ -444,14 +444,14 @@
             swap_ga.wait_send()
             swap_gb.wait_send()
 
-    def layer(gr, ch):
-        @pl.loop(0, 5)
-        def _(n):
-            off = pl.multiple_of(256 * n, 256)
-            acc = dot(hs[512 * gr : 512 * gr + 512, :], w[:, pl.ds(pl.multiple_of(1280 * ch + off, 256), 256)])
-            for tt in range(8):
-                r = 64 * (tt // 2)
-                lp[gr, ch, tt % 2, r : r + 64, pl.ds(off, 256)] = acc[64 * tt : 64 * tt + 64].astype(BF)
+    def layer(gr, ch, n):
+        off = 640 * n
+        acc = dot(hs[512 * gr : 512 * gr + 512, :], w[:, 1280 * ch + off : 1280 * ch + off + 640])
+        for tt in range(8):
+            r = 64 * (tt // 2)
+            lp[gr, ch, tt % 2, r : r + 64, off : off + 640] = acc[64 * tt : 64 * tt + 64].astype(BF)
+        if n == 1:
+            start(l_core[gr, ch])
 
     l_core, l_y1, l_y2, l_p = {}, {}, {}, {}
 
@@ -615,47 +615,47 @@
     for d in (1, -1):
         q_a[4, d].wait_recv()
     unpack(1 - vb)
-    layer(1, 0)
-    start(l_core[1, 0])
+    layer(1, 0, 0)
+    layer(1, 0, 1)
     rs_b(0, 2)
-    layer_core(1, 0)
-    rs_a(2, 1)
     dhidden(1, 1)
     d_send_p(1)
+    rs_a(2, 1)
+    layer_core(1, 0)
+    layer(1, 1, 0)
     rs_b(1, 3)
+    layer(1, 1, 1)
     rs_a(2, -1)
-    layer(1, 1)
-    start(l_core[1, 1])
+    dhidden(0, 0)
+    d_send_core(0)
+    layer_core(1, 1)
     rs_b(0, 3)
     layer_y(1, 0)
-    dhidden(0, 0)
-    d_send_core(0)
-    rs_a(3, 1)
-    layer_core(1, 1)
-    rs_b(1, 4)
-    rs_a(3, -1)
     dhidden(0, 1)
     d_send_core(1)
-    layer(0, 0)
-    start(l_core[0, 0])
+    rs_a(3, 1)
+    layer(0, 0, 0)
+    rs_b(1, 4)
+    layer(0, 0, 1)
+    rs_a(3, -1)
+    layer_y(1, 1)
+    layer(0, 1, 0)
     rs_b(0, 4)
-    layer_y(1, 1)
+    layer(0, 1, 1)
+    layer_core(0, 0)
     rs_a(4, 1)
-    layer(0, 1)
-    start(l_core[0, 1])
-    layer_core(0, 0)
-    rs_a(4, -1)
     layer_end(1, 0)
     rs_b_other()
+    rs_a(4, -1)
     layer_core(0, 1)
     layer_y(0, 0)
     layer_end(1, 1)
     rs_x(0)
+    rs_b_end()
     layer_y(0, 1)
+    rs_a_end()
     for q in (0, 1):
         d_recv(q)
-    rs_b_end()
-    rs_a_end()
     layer_end(0, 0)
     layer_end(0, 1)
     rs_end()

time: 92.5 us -> 90.1 us (0.974)
  Pallas kernels: 88.8 us -> 86.5 us
    pallas_call x1, Pallas kernels: 85.7 us -> 83.3 us  [body(): pl.pallas_call(kernel, out_shape=(jax.ShapeDtypeStruct((64, D), BF), jax....]
where the time goes in v4:
time: 90.1 us; the launch traced here: 89.9 us
  Pallas kernels  86.5 us (96%)
  local copies, waits for them, and re-layouts  2.63 us (3%)
    pallas_call x1, Pallas kernels, body(): pl.pallas_call(kernel, out_shape=(jax.ShapeDtypeStruct((64, D), BF), jax....  83.3 us
    pallas_call x1, Pallas kernels, body(): pl.pallas_call(last_kernel, out_shape=(jax.ShapeDtypeStruct((UNITS, TOK),...  3.17 us
    unnamed x10, local copies, waits for them, and re-layouts  2.63 us

profile of v4, /device:TPU:1, one launch (start us, length us, event | category | flops | bytes accessed | tf_op | source)
XLA Modules:
  0.0 89.9 jit_solution(9609882333736611504)
XLA Ops:
  0.6 0.0 copy-start.2
  0.6 1.0 %copy-done.2 = bf16[64,2560]{1,0:T(8,128)(2,1)S(1)} copy-done((bf16[64,2560]{1,0:T(8,128)(2,1)S(1)}, bf16[64,2560]{1,0:T(8,128)(2,1)}, u32[]{:S(2)}) %copy-start.2) | copy-done | bytes 327704
  1.6 0.0 copy-start.3
  1.6 1.0 %copy-done.3 = bf16[50,2560]{1,0:T(8,128)(2,1)S(1)} copy-done((bf16[50,2560]{1,0:T(8,128)(2,1)S(1)}, bf16[50,2560]{1,0:T(8,128)(2,1)}, u32[]{:S(2)}) %copy-start.3) | copy-done | bytes 256024
  2.6 0.0 copy-start.4
  2.6 0.7 copy-done.4
  3.3 0.0 copy-start
  3.3 0.0 copy-start.1
  3.3 83.3 %shard_map.84 = (bf16[64,2560]{1,0:T(8,128)(2,1)S(1)}, bf16[1600,512]{1,0:T(8,128)(2,1)S(1)}, f32[1008,128]{1,0:T(8,128)S(1)}) custom-call(bf16[1600,512]{1,0:T(8,128)(2,1)} %bitcast.5, bf16[1600,512]{1,0:T(8,128)(2,1)} %bitcast.7, bf16[50,2560]{1,0:T(8,128)(2,1)S(1)} %copy-done.3, f32[10,50]{1,0:T(8,128)S(1)} %bitcast.9, bf16[64,2560]{1,0:T(8,128)(2,1)S(1)} %copy-done.2), custom_call_target="tpu_custom_call" | custom-call | flops 24999999488 | bytes 10000000 | tf_op jit(solution)/shard_map/pallas_call | solution.py:717
  86.5 0.0 copy-done
  86.6 0.0 copy-done.1
  86.6 3.2 %shard_map.85 = (bf16[1600,512]{1,0:T(8,128)(2,1)}, bf16[1600,512]{1,0:T(8,128)(2,1)}, bf16[64,2560]{1,0:T(8,128)(2,1)}, f32[50,2560]{1,0:T(8,128)}) custom-call(bf16[1600,512]{1,0:T(8,128)(2,1)S(1)} %get-tuple-element.11.dr, bf16[1600,512]{1,0:T(8,128)(2,1)S(1)} %bitcast.6, bf16[1600,512]{1,0:T(8,128)(2,1)S(1)} %bitcast.8, ...), custom_call_target="tpu_custom_call" | custom-call | flops 20000000 | bytes 10000000 | tf_op jit(solution)/shard_map/pallas_call | solution.py:764
Async XLA Ops:
  0.6 1.0 %copy-start.2 = (bf16[64,2560]{1,0:T(8,128)(2,1)S(1)}, bf16[64,2560]{1,0:T(8,128)(2,1)}, u32[]{:S(2)}) copy-start(bf16[64,2560]{1,0:T(8,128)(2,1)} %cot_hbm.1) | copy-start | bytes 983044
  1.6 1.0 %copy-start.3 = (bf16[50,2560]{1,0:T(8,128)(2,1)S(1)}, bf16[50,2560]{1,0:T(8,128)(2,1)}, u32[]{:S(2)}) copy-start(bf16[50,2560]{1,0:T(8,128)(2,1)} %codes_hbm.1) | copy-start | bytes 768004
  2.6 0.7 copy-start.4
  3.3 83.3 %copy-start = (bf16[512,1600]{0,1:T(8,128)(2,1)S(1)}, bf16[512,1600]{0,1:T(8,128)(2,1)}, u32[]{:S(2)}) copy-start(bf16[512,1600]{0,1:T(8,128)(2,1)} %param.5) | copy-start | bytes 4915204
  3.3 83.3 %copy-start.1 = (bf16[512,1600]{0,1:T(8,128)(2,1)S(1)}, bf16[512,1600]{0,1:T(8,128)(2,1)}, u32[]{:S(2)}) copy-start(bf16[512,1600]{0,1:T(8,128)(2,1)} %param.6) | copy-start | bytes 4915204

commit v5 on v4

--- a/solution.py
+++ b/solution.py
@@ -513,9 +513,10 @@
             d_core[h, q] = rc(src, dr.at[drows(h, q)], core)
             d_own[h, q] = pltpu.make_async_copy(src, dr.at[drows(h, q)], lsem.at[5 + q])
 
-    def dhidden(gr, o):
+    def dhidden(gr, o, k):
         r = rows_at(half_of(o))
-        dd[gr, r, :] = dot_nt(w[r, :], cot[512 * gr : 512 * gr + 512, :]).astype(BF)
+        lo = 256 * k
+        dd[gr, r, lo : lo + 256] = dot_nt(w[r, :], cot[512 * gr + lo : 512 * gr + lo + 256, :]).astype(BF)
 
     def d_send_p(q):
         @pl.when(is_r)
@@ -604,7 +605,8 @@
     rs_begin(0)
     ag_b(4, fb_own)
     unpack(vb)
-    dhidden(1, 0)
+    dhidden(1, 0, 0)
+    dhidden(1, 0, 1)
     d_send_p(0)
     rs_b(1, 2)
     ag_b(4, fb_q)
@@ -618,22 +620,25 @@
     layer(1, 0, 0)
     layer(1, 0, 1)
     rs_b(0, 2)
-    dhidden(1, 1)
+    dhidden(1, 1, 0)
+    rs_a(2, 1)
+    dhidden(1, 1, 1)
     d_send_p(1)
-    rs_a(2, 1)
     layer_core(1, 0)
     layer(1, 1, 0)
     rs_b(1, 3)
     layer(1, 1, 1)
     rs_a(2, -1)
-    dhidden(0, 0)
-    d_send_core(0)
+    dhidden(0, 0, 0)
     layer_core(1, 1)
     rs_b(0, 3)
+    dhidden(0, 0, 1)
+    d_send_core(0)
     layer_y(1, 0)
-    dhidden(0, 1)
+    dhidden(0, 1, 0)
+    rs_a(3, 1)
+    dhidden(0, 1, 1)
     d_send_core(1)
-    rs_a(3, 1)
     layer(0, 0, 0)
     rs_b(1, 4)
     layer(0, 0, 1)

time: 90.1 us -> 90.9 us (level)
  no operation moved by 1% of the time
where the time goes in v5:
time: 90.9 us; the launch traced here: 90.7 us
  Pallas kernels  87.3 us (96%)
  local copies, waits for them, and re-layouts  2.63 us (3%)
    pallas_call x1, Pallas kernels, body(): pl.pallas_call(kernel, out_shape=(jax.ShapeDtypeStruct((64, D), BF), jax....  84.1 us
    pallas_call x1, Pallas kernels, body(): pl.pallas_call(last_kernel, out_shape=(jax.ShapeDtypeStruct((UNITS, TOK),...  3.17 us
    unnamed x10, local copies, waits for them, and re-layouts  2.63 us

profile of v5, /device:TPU:1, one launch (start us, length us, event | category | flops | bytes accessed | tf_op | source)
XLA Modules:
  0.0 90.7 jit_solution(9613205943184783966)
XLA Ops:
  0.6 0.0 copy-start.2
  0.6 1.0 %copy-done.2 = bf16[64,2560]{1,0:T(8,128)(2,1)S(1)} copy-done((bf16[64,2560]{1,0:T(8,128)(2,1)S(1)}, bf16[64,2560]{1,0:T(8,128)(2,1)}, u32[]{:S(2)}) %copy-start.2) | copy-done | bytes 327704
  1.6 0.0 copy-start.3
  1.6 1.0 %copy-done.3 = bf16[50,2560]{1,0:T(8,128)(2,1)S(1)} copy-done((bf16[50,2560]{1,0:T(8,128)(2,1)S(1)}, bf16[50,2560]{1,0:T(8,128)(2,1)}, u32[]{:S(2)}) %copy-start.3) | copy-done | bytes 256024
  2.6 0.0 copy-start.4
  2.6 0.7 copy-done.4
  3.3 0.0 copy-start
  3.3 0.0 copy-start.1
  3.3 84.1 %shard_map.84 = (bf16[64,2560]{1,0:T(8,128)(2,1)S(1)}, bf16[1600,512]{1,0:T(8,128)(2,1)S(1)}, f32[1008,128]{1,0:T(8,128)S(1)}) custom-call(bf16[1600,512]{1,0:T(8,128)(2,1)} %bitcast.5, bf16[1600,512]{1,0:T(8,128)(2,1)} %bitcast.7, bf16[50,2560]{1,0:T(8,128)(2,1)S(1)} %copy-done.3, f32[10,50]{1,0:T(8,128)S(1)} %bitcast.9, bf16[64,2560]{1,0:T(8,128)(2,1)S(1)} %copy-done.2), custom_call_target="tpu_custom_call" | custom-call | flops 24999999488 | bytes 10000000 | tf_op jit(solution)/shard_map/pallas_call | solution.py:722
  87.4 0.0 copy-done
  87.4 0.0 copy-done.1
  87.4 3.2 %shard_map.85 = (bf16[1600,512]{1,0:T(8,128)(2,1)}, bf16[1600,512]{1,0:T(8,128)(2,1)}, bf16[64,2560]{1,0:T(8,128)(2,1)}, f32[50,2560]{1,0:T(8,128)}) custom-call(bf16[1600,512]{1,0:T(8,128)(2,1)S(1)} %get-tuple-element.11.dr, bf16[1600,512]{1,0:T(8,128)(2,1)S(1)} %bitcast.6, bf16[1600,512]{1,0:T(8,128)(2,1)S(1)} %bitcast.8, ...), custom_call_target="tpu_custom_call" | custom-call | flops 20000000 | bytes 10000000 | tf_op jit(solution)/shard_map/pallas_call | solution.py:769
Async XLA Ops:
  0.6 1.0 %copy-start.2 = (bf16[64,2560]{1,0:T(8,128)(2,1)S(1)}, bf16[64,2560]{1,0:T(8,128)(2,1)}, u32[]{:S(2)}) copy-start(bf16[64,2560]{1,0:T(8,128)(2,1)} %cot_hbm.1) | copy-start | bytes 983044
  1.6 1.0 %copy-start.3 = (bf16[50,2560]{1,0:T(8,128)(2,1)S(1)}, bf16[50,2560]{1,0:T(8,128)(2,1)}, u32[]{:S(2)}) copy-start(bf16[50,2560]{1,0:T(8,128)(2,1)} %codes_hbm.1) | copy-start | bytes 768004
  2.6 0.7 copy-start.4
  3.3 84.1 %copy-start = (bf16[512,1600]{0,1:T(8,128)(2,1)S(1)}, bf16[512,1600]{0,1:T(8,128)(2,1)}, u32[]{:S(2)}) copy-start(bf16[512,1600]{0,1:T(8,128)(2,1)} %param.5) | copy-start | bytes 4915204
  3.3 84.1 %copy-start.1 = (bf16[512,1600]{0,1:T(8,128)(2,1)S(1)}, bf16[512,1600]{0,1:T(8,128)(2,1)}, u32[]{:S(2)}) copy-start(bf16[512,1600]{0,1:T(8,128)(2,1)} %param.6) | copy-start | bytes 4915204
